TPU v7x, 32 devices: a whole 2x2x4 slice. The times are simulated.
32 devices in a mesh: tm: 8 (over y, x, core), batch: 4 (over z).
Axes of the slice: x: 2, y: 2, z: 4, core: 2. Of those that a mesh axis runs over, the one named last changes fastest.
Arguments:
- audio: bfloat16 [4, 24576, 512], P('batch', 'tm'), may hold values from -6 to 6
- conditioning: bfloat16 [4, 80, 24576], P('batch', None, 'tm'), may hold values from -6 to 6
- speaker_ids: int32 [4, 8], P('batch'), may hold values from 0 to 111
- seg_starts: int32 [4, 8], P('batch'), may hold values from 0 to 24575, as said below
- grad_residual: bfloat16 [4, 24576, 512], P('batch', 'tm'), may hold values from -6 to 6
- grad_skip: bfloat16 [4, 24576, 512], P('batch', 'tm'), may hold values from -6 to 6
- conv_weight: float32 [1024, 1024], P('batch', 'tm'), may hold values from -0.1875 to 0.1875
- conv_first: float32 [1024, 1024], P('batch', 'tm'), may hold values from -0.0014648438 to 0.0014648438
- conv_second: float32 [1024, 1024], P('batch', 'tm'), may hold values from 8.58894e-10 to 3.435576e-09
- cond_weight: float32 [80, 1024], P('batch', 'tm'), may hold values from -0.625 to 0.625
- cond_first: float32 [80, 1024], P('batch', 'tm'), may hold values from -0.0014648438 to 0.0014648438
- cond_second: float32 [80, 1024], P('batch', 'tm'), may hold values from 8.58894e-10 to 3.435576e-09
- speaker_table: float32 [112, 1024], P('batch', 'tm'), may hold values from -1.5 to 1.5
- table_first: float32 [112, 1024], P('batch', 'tm'), may hold values from -0.00015258789 to 0.00015258789
- table_second: float32 [112, 1024], P('batch', 'tm'), may hold values from 7.668696e-12 to 3.0674786e-11
- out_weight: float32 [512, 1024], P('batch', 'tm'), may hold values from -0.75 to 0.75
- out_first: float32 [512, 1024], P('batch', 'tm'), may hold values from -0.00036621094 to 0.00036621094
- out_second: float32 [512, 1024], P('batch', 'tm'), may hold values from 5.3680876e-11 to 2.147235e-10
Outputs:
- residual_out: bfloat16 [4, 24576, 512], P('batch', 'tm')
- skip_out: bfloat16 [4, 24576, 512], P('batch', 'tm')
- audio_grad: bfloat16 [4, 24576, 512], P('batch', 'tm')
- prenorm: float32 [], replicated
- conv_first_new: float32 [1024, 1024], P('batch', 'tm')
- conv_second_new: float32 [1024, 1024], P('batch', 'tm')
- conv_new: float32 [1024, 1024], P('batch', 'tm')
- cond_first_new: float32 [80, 1024], P('batch', 'tm')
- cond_second_new: float32 [80, 1024], P('batch', 'tm')
- cond_new: float32 [80, 1024], P('batch', 'tm')
- table_first_new: float32 [112, 1024], P('batch', 'tm')
- table_second_new: float32 [112, 1024], P('batch', 'tm')
- table_new: float32 [112, 1024], P('batch', 'tm')
- out_first_new: float32 [512, 1024], P('batch', 'tm')
- out_second_new: float32 [512, 1024], P('batch', 'tm')
- out_new: float32 [512, 1024], P('batch', 'tm')
Inputs may be any that keep to these rules, and one draw needn't show every extreme that they name: `seg_starts`: each row's starts rise strictly from 0 at the first; the segment that begins at the second start holds samples of the first 3072 and of the last 3072 of its row.
All inputs are finite; a program needn't handle non-finite values.
Results may differ from a plain program's by a relative error of at most 0.0067.
Values may be sent and summed in bfloat16 or wider, within the bound.
A program may use at most 192 MiB of HBM per device.

v0:
```python
import jax
import jax.numpy as jnp
from jax import lax
from jax.sharding import PartitionSpec as P

DILATION_SIZE = 256
STEP = 10


clip_level = 1.0
beta_one = 0.9
beta_two = 0.999
adam_eps = 1e-08
decay_rate = 0.01
learn_rate = 0.1


def passed_along(value, axis, steps):
    count = lax.axis_size(axis)
    first, last = (max(0, -steps), min(count, count - steps))
    return lax.ppermute(value, axis, [(source, source + steps) for source in range(first, last)])


def contract_rows(left, right):
    return lax.dot_general(
        left, right, (((0,), (0,)), ((), ())), preferred_element_type=jnp.float32
    )


def contract_cols(left, right):
    return lax.dot_general(
        left, right, (((1,), (1,)), ((), ())), preferred_element_type=jnp.float32
    )


def own_block(whole, shard):
    row_start = lax.axis_index("batch") * shard.shape[0]
    col_start = lax.axis_index("tm") * shard.shape[1]
    return lax.dynamic_slice(whole, (row_start, col_start), shard.shape)


def square_sum(matrix):
    return jnp.sum(matrix * matrix)


def adamw(gradient, factor, master, first_old, second_old):
    clipped = gradient * factor
    new_first = beta_one * first_old + (1.0 - beta_one) * clipped
    new_second = beta_two * second_old + (1.0 - beta_two) * clipped * clipped
    step_size = (
        new_first
        / (1.0 - beta_one**STEP)
        / (jnp.sqrt(new_second / (1.0 - beta_two**STEP)) + adam_eps)
    )
    new_master = master - learn_rate * (step_size + decay_rate * master)
    return (new_first, new_second, new_master)


def on_device(
    audio,
    conditioning,
    speaker_ids,
    seg_starts,
    grad_residual,
    grad_skip,
    conv_weight,
    conv_first,
    conv_second,
    cond_weight,
    cond_first,
    cond_second,
    speaker_table,
    table_first,
    table_second,
    out_weight,
    out_first,
    out_second,
):
    rows_dev, steps_per_device, channels = audio.shape
    tokens = rows_dev * steps_per_device
    conv_rows, cond_rows, table_rows, out_rows = (
        lax.all_gather(conv_weight.astype(jnp.bfloat16), "batch", axis=0, tiled=True),
        lax.all_gather(cond_weight.astype(jnp.bfloat16), "batch", axis=0, tiled=True),
        lax.all_gather(speaker_table.astype(jnp.bfloat16), "batch", axis=0, tiled=True),
        lax.all_gather(out_weight.astype(jnp.bfloat16), "batch", axis=0, tiled=True),
    )
    conv_full, cond_full, table_full, out_full = (
        lax.all_gather(conv_rows, "tm", axis=1, tiled=True),
        lax.all_gather(cond_rows, "tm", axis=1, tiled=True),
        lax.all_gather(table_rows, "tm", axis=1, tiled=True),
        lax.all_gather(out_rows, "tm", axis=1, tiled=True),
    )
    offset = lax.axis_index("tm") * steps_per_device
    positions = offset + jnp.arange(steps_per_device, dtype=jnp.int32)
    seg_count = seg_starts.shape[1]
    segment = (
        jnp.sum((positions[None, :, None] >= seg_starts[:, None, :]).astype(jnp.int32), axis=2) - 1
    )
    seg_match = segment[:, :, None] == jnp.arange(seg_count, dtype=jnp.int32)[None, None, :]
    local_start = jnp.sum(jnp.where(seg_match, seg_starts[:, None, :], 0), axis=2)
    retain_mask = (positions[None, :] - DILATION_SIZE >= local_start).astype(jnp.bfloat16)
    seg_hot = seg_match.astype(jnp.bfloat16)
    speakers = table_full.shape[0]
    speaker_hot = (
        speaker_ids[:, :, None] == jnp.arange(speakers, dtype=jnp.int32)[None, None, :]
    ).astype(jnp.bfloat16)
    seg_embed = jnp.einsum(
        "rsk,kf->rsf", speaker_hot, table_full, preferred_element_type=jnp.float32
    ).astype(jnp.bfloat16)
    tail_input = passed_along(audio[:, steps_per_device - DILATION_SIZE :, :], "tm", 1)
    previous = (
        jnp.concatenate([tail_input, audio[:, : steps_per_device - DILATION_SIZE, :]], axis=1)
        * retain_mask[:, :, None]
    )
    flat_audio = audio.reshape(tokens, channels)
    flat_prev = previous.reshape(tokens, channels)
    mixture = jnp.dot(flat_prev, conv_full[:channels], preferred_element_type=jnp.float32)
    mixture = mixture + jnp.dot(
        flat_audio, conv_full[channels:], preferred_element_type=jnp.float32
    )
    mixture = mixture + jnp.einsum(
        "rct,cf->rtf", conditioning, cond_full, preferred_element_type=jnp.float32
    ).reshape(tokens, -1)
    mixture = mixture + jnp.einsum(
        "rts,rsf->rtf", seg_hot, seg_embed, preferred_element_type=jnp.float32
    ).reshape(tokens, -1)
    filter_tanh = jnp.tanh(mixture[:, :channels])
    gate_sig = jax.nn.sigmoid(mixture[:, channels:])
    gated_out = (filter_tanh * gate_sig).astype(jnp.bfloat16)
    projected = jnp.dot(gated_out, out_full, preferred_element_type=jnp.float32)
    residual_out = (
        (flat_audio.astype(jnp.float32) + projected[:, :channels])
        .astype(jnp.bfloat16)
        .reshape(audio.shape)
    )
    skip_out = projected[:, channels:].astype(jnp.bfloat16).reshape(audio.shape)
    back_out = jnp.concatenate(
        [grad_residual.reshape(tokens, channels), grad_skip.reshape(tokens, channels)], axis=1
    )
    out_grad = contract_rows(gated_out, back_out)
    gated_grad = contract_cols(back_out, out_full)
    filter_grad = gated_grad * gate_sig * (1.0 - filter_tanh * filter_tanh)
    gate_grad = gated_grad * filter_tanh * gate_sig * (1.0 - gate_sig)
    mixture_grad = jnp.concatenate([filter_grad, gate_grad], axis=1).astype(jnp.bfloat16)
    conv_grad = jnp.concatenate(
        [contract_rows(flat_prev, mixture_grad), contract_rows(flat_audio, mixture_grad)], axis=0
    )
    grad_blocks = mixture_grad.reshape(rows_dev, steps_per_device, -1)
    cond_grad = jnp.einsum(
        "rct,rtf->cf", conditioning, grad_blocks, preferred_element_type=jnp.float32
    )
    seg_sums = jnp.einsum("rts,rtf->rsf", seg_hot, grad_blocks, preferred_element_type=jnp.float32)
    table_grad = jnp.einsum(
        "rsk,rsf->kf",
        speaker_hot.astype(jnp.float32),
        seg_sums,
        precision=lax.Precision.HIGHEST,
        preferred_element_type=jnp.float32,
    )
    preceding_gradient = (
        contract_cols(mixture_grad, conv_full[:channels]).reshape(audio.shape)
        * retain_mask[:, :, None]
    ).astype(jnp.bfloat16)
    head_input = passed_along(preceding_gradient[:, :DILATION_SIZE, :], "tm", -1)
    later_contribution = jnp.concatenate(
        [preceding_gradient[:, DILATION_SIZE:, :], head_input], axis=1
    ).astype(jnp.float32)
    current_tap = contract_cols(mixture_grad, conv_full[channels:]).reshape(audio.shape)
    audio_grad = (grad_residual.astype(jnp.float32) + current_tap + later_contribution).astype(
        jnp.bfloat16
    )
    conv_total, cond_total, table_total, out_total = lax.psum(
        (conv_grad, cond_grad, table_grad, out_grad), ("tm", "batch")
    )
    squares = (
        square_sum(conv_total)
        + square_sum(cond_total)
        + square_sum(table_total)
        + square_sum(out_total)
    )
    conv_part = own_block(conv_total, conv_weight)
    cond_part = own_block(cond_total, cond_weight)
    table_part = own_block(table_total, speaker_table)
    out_part = own_block(out_total, out_weight)
    prenorm = jnp.sqrt(squares)
    factor = jnp.minimum(1.0, clip_level / (prenorm + 1e-06))
    conv_state = adamw(conv_part, factor, conv_weight, conv_first, conv_second)
    cond_state = adamw(cond_part, factor, cond_weight, cond_first, cond_second)
    table_state = adamw(table_part, factor, speaker_table, table_first, table_second)
    out_state = adamw(out_part, factor, out_weight, out_first, out_second)
    return (
        residual_out,
        skip_out,
        audio_grad,
        prenorm,
        conv_state[0],
        conv_state[1],
        conv_state[2],
        cond_state[0],
        cond_state[1],
        cond_state[2],
        table_state[0],
        table_state[1],
        table_state[2],
        out_state[0],
        out_state[1],
        out_state[2],
    )


def solution(mesh):
    placed = (
        P("batch", "tm", None),
        P("batch", None, "tm"),
        P("batch", None),
        P("batch", None),
        P("batch", "tm", None),
        P("batch", "tm", None),
        P("batch", "tm"),
        P("batch", "tm"),
        P("batch", "tm"),
        P("batch", "tm"),
        P("batch", "tm"),
        P("batch", "tm"),
        P("batch", "tm"),
        P("batch", "tm"),
        P("batch", "tm"),
        P("batch", "tm"),
        P("batch", "tm"),
        P("batch", "tm"),
    )
    return jax.shard_map(
        on_device,
        mesh=mesh,
        in_specs=placed,
        out_specs=(
            P("batch", "tm", None),
            P("batch", "tm", None),
            P("batch", "tm", None),
            P(),
            P("batch", "tm"),
            P("batch", "tm"),
            P("batch", "tm"),
            P("batch", "tm"),
            P("batch", "tm"),
            P("batch", "tm"),
            P("batch", "tm"),
            P("batch", "tm"),
            P("batch", "tm"),
            P("batch", "tm"),
            P("batch", "tm"),
            P("batch", "tm"),
        ),
        check_vma=False,
    )
```

profile of v0, /device:TPU:0, one launch (start us, length us, event | category | flops | bytes accessed | tf_op | source)
XLA Modules:
  0.0 368.1 jit_solution(2074321143572299324)
XLA Ops:
  8.2 16.3 %all_gather.24 = bf16[1024,128]{1,0:T(8,128)(2,1)} all-gather(bf16[256,128]{1,0:T(8,128)(2,1)S(1)} %convert_element_type.91), channel_id=1, replica_groups=mesh['tm'=8,'batch'=4] {'batch'}, dimensions={0}, use_global_device_ids=true | all-gather | bytes 327680 | tf_op jit(solution)/shard_map/all_gather | solution.py:82
  29.1 14.5 %all_gather.30 = bf16[512,128]{1,0:T(8,128)(2,1)} all-gather(bf16[128,128]{1,0:T(8,128)(2,1)S(1)} %convert_element_type.96), channel_id=1, replica_groups=mesh['tm'=8,'batch'=4] {'batch'}, dimensions={0}, use_global_device_ids=true | all-gather | bytes 163840 | tf_op jit(solution)/shard_map/all_gather | solution.py:85
  43.7 2.3 slice_bitcast_fusion
  46.9 13.1 %all-gather.1 = bf16[4,28,128]{2,1,0:T(8,128)(2,1)S(1)} all-gather(bf16[1,28,128]{2,1,0:T(8,128)(2,1)S(1)} %convert_bitcast_fusion), channel_id=1, replica_groups=mesh['tm'=8,'batch'=4] {'batch'}, dimensions={0}, use_global_device_ids=true | all-gather | bytes 35840 | tf_op jit(solution)/shard_map/all_gather | solution.py:84
  60.0 10.3 %all_gather.29 = bf16[112,1024]{1,0:T(8,128)(2,1)} all-gather(bf16[112,128]{1,0:T(8,128)(2,1)S(1)} %reshape.365), channel_id=1, replica_groups=mesh['tm'=8,'batch'=4] {'tm'}, dimensions={1}, use_global_device_ids=true | all-gather | bytes 258048 | tf_op jit(solution)/shard_map/all_gather | solution.py:90
  70.3 13.1 %all-gather = bf16[4,20,128]{2,1,0:T(8,128)(2,1)S(1)} all-gather(bf16[1,20,128]{2,1,0:T(8,128)(2,1)S(1)} %convert_bitcast_fusion.1), channel_id=1, replica_groups=mesh['tm'=8,'batch'=4] {'batch'}, dimensions={0}, use_global_device_ids=true | all-gather | bytes 25600 | tf_op jit(solution)/shard_map/all_gather | solution.py:83
  84.1 8.8 %all_gather.27 = bf16[80,1024]{1,0:T(8,128)(2,1)S(1)} all-gather(bf16[80,128]{1,0:T(8,128)(2,1)} %reshape.363), channel_id=1, replica_groups=mesh['tm'=8,'batch'=4] {'tm'}, dimensions={1}, use_global_device_ids=true | all-gather | bytes 184320 | tf_op jit(solution)/shard_map/all_gather | solution.py:89
  92.8 7.4 %fusion.21 = f32[3072,1024]{0,1:T(8,128)} fusion(bf16[112,1024]{1,0:T(8,128)(2,1)} %all_gather.29, s32[3072]{0:T(1024)S(1)} %broadcast_add_fusion, s32[8]{0:T(128)S(1)} %bitcast.49), kind=kOutput, calls=%fused_computation.38 | convolution fusion | flops 52200320 | bytes 12824608 | tf_op jit(solution)/shard_map/rts,rsf->rtf/dot_general | solution.py:124
  100.3 6.4 %fusion.30 = f32[3072,1024]{0,1:T(8,128)} fusion(bf16[80,1024]{1,0:T(8,128)(2,1)S(1)} %all_gather.27, bf16[1,80,3072]{2,1,0:T(8,128)(2,1)S(1)} %copy-done), kind=kOutput, calls=%fused_computation.45 | convolution fusion | flops 503316480 | bytes 13238272 | tf_op jit(solution)/shard_map/rct,cf->rtf/dot_general | solution.py:121
  106.6 10.3 %fusion.13 = f32[3072,1024]{0,1:T(8,128)} fusion(bf16[1,3072,512]{2,1,0:T(8,128)(2,1)} %param.18, bf16[1024,1024]{1,0:T(8,128)(2,1)} %all-gather.5.cloned.1.call-done), kind=kOutput, calls=%fused_computation.28 | convolution fusion | flops 3221225472 | bytes 16777216 | tf_op jit(solution)/shard_map/dot_general | solution.py:118
  116.9 20.0 %add_add_fusion = f32[3072,1024]{0,1:T(8,128)} fusion(f32[3072,1024]{0,1:T(8,128)} %fusion.21, f32[3072,1024]{0,1:T(8,128)} %fusion.30, f32[3072,1024]{0,1:T(8,128)} %fusion.13, bf16[2816,512]{1,0:T(8,128)(2,1)S(1)} %slice_bitcast_fusion, bf16[256,512]{1,0:T(8,128)(2,1)} %bitcast.1, bf16[3072]{0:T(1024)(128)(2,1)S(1)} %copy-done.16, ...), kind=kOutput, calls=%fused_computation | convolution fusion | flops 3240099840 | bytes 54532096 | tf_op jit(solution)/shard_map/dot_general | solution.py:117
  136.9 10.4 %multiply_convert_fusion.2 = (bf16[3072,512]{0,1:T(8,128)(2,1)S(1)}, bf16[3072,512]{0,1:T(8,128)(2,1)S(1)}, bf16[3072,512]{0,1:T(8,128)(2,1)S(1)}) fusion(f32[3072,1024]{0,1:T(8,128)} %add_add_fusion, bf16[512,1024]{1,0:T(8,128)(2,1)} %all-gather.7.cloned.1.call-done, bf16[3072,512]{1,0:T(8,128)(2,1)} %bitcast.51, bf16[3072,512]{1,0:T(8,128)(2,1)} %bitcast.53), kind=kOutput, calls=%fused_computation.16 | convolution fusion | flops 3257401344 | bytes 29360128 | tf_op jit(solution)/shard_map/dot_general | solution.py:31
  147.3 5.5 %fusion.15 = f32[512,1024]{1,0:T(8,128)S(1)} fusion(bf16[2816,512]{1,0:T(8,128)(2,1)S(1)} %slice_bitcast_fusion, bf16[256,512]{1,0:T(8,128)(2,1)} %bitcast.1, bf16[3072]{0:T(1024)(128)(2,1)S(1)} %copy-done.16, bf16[3072,512]{0,1:T(8,128)(2,1)S(1)} %get-tuple-element.35, bf16[3072,512]{0,1:T(8,128)(2,1)S(1)} %get-tuple-element.34), kind=kOutput, calls=%fused_computation.32 | convolution fusion | flops 3243245568 | bytes 11540480 | tf_op jit(solution)/shard_map/dot_general | solution.py:25
  152.9 3.5 fusion.16
  158.1 2.8 convolution_bitcast_fusion
  162.2 5.0 %fusion.7 = f32[512,1024]{1,0:T(8,128)} fusion(bf16[3072,512]{0,1:T(8,128)(2,1)S(1)} %get-tuple-element.36, bf16[3072,512]{1,0:T(8,128)(2,1)S(1)} %bitcast.52, bf16[3072,512]{1,0:T(8,128)(2,1)S(1)} %bitcast.54), kind=kOutput, calls=%fused_computation.21 | convolution fusion | flops 3233808384 | bytes 11534336 | tf_op jit(solution)/shard_map/dot_general | solution.py:25
  167.2 4.0 %fusion.6 = bf16[1,3072,512]{2,1,0:T(8,128)(2,1)S(1)} fusion(f32[3072]{0:T(1024)S(1)} %copy-done.19, bf16[1024,1024]{1,0:T(8,128)(2,1)S(1)} %copy-done.5, bf16[3072,512]{0,1:T(8,128)(2,1)S(1)} %get-tuple-element.35, bf16[3072,512]{0,1:T(8,128)(2,1)S(1)} %get-tuple-element.34), kind=kOutput, calls=%fused_computation.20 | convolution fusion | flops 3236954112 | bytes 10498048 | tf_op jit(solution)/shard_map/dot_general | solution.py:31
  174.2 2.3 pad_maximum_fusion.2
  176.6 5.8 %fusion.54 = f32[3072,1024]{1,0:T(8,128)S(1)} fusion(bf16[3072,512]{0,1:T(8,128)(2,1)} %copy-done.27, bf16[512,1024]{1,0:T(8,128)(2,1)} %all-gather.7.cloned.1.call-done), kind=kOutput, calls=%fused_computation.91 | convolution fusion | flops 3221225472 | bytes 16777216 | tf_op jit(solution)/shard_map/dot_general | solution.py:130
  182.4 2.8 fusion.9
  185.2 2.2 fusion.10
  190.1 7.7 %fusion.5 = bf16[1,3072,512]{2,1,0:T(8,128)(2,1)} fusion(bf16[1,3072,512]{2,1,0:T(8,128)(2,1)S(1)} %copy-done.26, bf16[1,256,512]{2,1,0:T(8,128)(2,1)S(1)} %collective-permute-done.1, bf16[1,2816,512]{2,1,0:T(8,128)(2,1)S(1)} %slice-done, bf16[1024,1024]{1,0:T(8,128)(2,1)S(1)} %copy-done.5, bf16[3072,512]{0,1:T(8,128)(2,1)} %copy-done.30, ...), kind=kOutput, calls=%fused_computation.13 | convolution fusion | flops 3246391296 | bytes 16777216 | tf_op jit(solution)/shard_map/dot_general | solution.py:31
  197.9 145.5 %all-reduce.3.cloned.1.call-done = (f32[1024,1024]{1,0:T(8,128)}, f32[80,1024]{1,0:T(8,128)}, f32[112,1024]{1,0:T(8,128)}, f32[512,1024]{1,0:T(8,128)}) async-done(((f32[1024,1024]{1,0:T(8,128)}, f32[80,1024]{1,0:T(8,128)}, f32[112,1024]{1,0:T(8,128)}, f32[512,1024]{1,0:T(8,128)}), (f32[1024,1024]{1,0:T(8,128)}, f32[80,1024]{1,0:T(8,128)}, f32[112,1024]{1,0:T(8,128)}, ...) | async-done | bytes 7077904 | tf_op jit(solution)/shard_map/psum | solution.py:172
  343.4 4.0 %multiply_reduce_fusion = f32[]{:T(128)} fusion(f32[1024,1024]{1,0:T(8,128)} %get-tuple-element.16), kind=kLoop, calls=%fused_computation.19 | loop fusion | flops 2097151 | bytes 4194308 | tf_op jit(solution)/shard_map/reduce_sum | solution.py:43
  (98 shorter events, 25.7 us)
Async XLA Ops:
  7.2 93.1 %copy-start = (bf16[1,80,3072]{2,1,0:T(8,128)(2,1)S(1)}, bf16[1,80,3072]{2,1,0:T(8,128)(2,1)}, u32[]{:S(2)}) copy-start(bf16[1,80,3072]{2,1,0:T(8,128)(2,1)} %param.19) | copy-start | bytes 1474564
  7.2 38.8 %copy-start.22 = (s32[1,8]{1,0:T(1,128)S(1)}, s32[1,8]{1,0:T(1,128)}, u32[]{:S(2)}) copy-start(s32[1,8]{1,0:T(1,128)} %param.21) | copy-start | bytes 100
  7.2 39.6 %copy-start.10 = (f32[28,128]{1,0:T(8,128)S(1)}, f32[28,128]{1,0:T(8,128)}, u32[]{:S(2)}) copy-start(f32[28,128]{1,0:T(8,128)} %param.30) | copy-start | bytes 43012
  7.2 63.1 %copy-start.14 = (f32[20,128]{1,0:T(8,128)S(1)}, f32[20,128]{1,0:T(8,128)}, u32[]{:S(2)}) copy-start(f32[20,128]{1,0:T(8,128)} %param.27) | copy-start | bytes 30724
  7.2 85.6 %copy-start.23 = (s32[1,8]{1,0:T(1,128)S(1)}, s32[1,8]{1,0:T(1,128)}, u32[]{:S(2)}) copy-start(s32[1,8]{1,0:T(1,128)} %param.20) | copy-start | bytes 100
  7.2 99.4 %all-gather.5.cloned.1.call-start = ((), (), s32[]{:S(2)}) async-start(), calls=%async_computation | async-start | bytes 2359296 | tf_op jit(solution)/shard_map/all_gather | solution.py:88
  24.6 112.3 %all-gather.7.cloned.1.call-start = ((), (), s32[]{:S(2)}) async-start(), calls=%async_computation.1 | async-start | bytes 1179648 | tf_op jit(solution)/shard_map/all_gather | solution.py:91
  26.3 90.6 %collective-permute-start = (bf16[1,256,512]{2,1,0:T(8,128)(2,1)}, bf16[1,256,512]{2,1,0:T(8,128)(2,1)}, u32[]{:S(2)}, u32[]{:S(2)}) collective-permute-start(bf16[1,256,512]{2,1,0:T(8,128)(2,1)} %slice.33), channel_id=1, source_target_pairs={{0,4},{4,8},{8,12},{12,16},{16,20},{20,24},{24,28},{1,5},{5,9},{9,... | collective-permute-start | bytes 786440 | tf_op jit(solution)/shard_map/ppermute | solution.py:21
  43.7 299.7 %all-reduce.3.cloned.1.call-start = ((), (), s32[]{:S(2)}) async-start(), calls=%async_computation.2 | async-start | bytes 14155776 | tf_op jit(solution)/shard_map/psum | solution.py:172
  147.3 19.9 %copy-start.28 = (bf16[3072,512]{0,1:T(8,128)(2,1)}, bf16[3072,512]{0,1:T(8,128)(2,1)S(1)}, u32[]{:S(2)}) copy-start(bf16[3072,512]{0,1:T(8,128)(2,1)S(1)} %get-tuple-element.34) | copy-start | bytes 9437188
  147.3 19.9 %copy-start.30 = (bf16[3072,512]{0,1:T(8,128)(2,1)}, bf16[3072,512]{0,1:T(8,128)(2,1)S(1)}, u32[]{:S(2)}) copy-start(bf16[3072,512]{0,1:T(8,128)(2,1)S(1)} %get-tuple-element.35) | copy-start | bytes 9437188
  172.9 14.5 %collective-permute-start.1 = (bf16[1,256,512]{2,1,0:T(8,128)(2,1)S(1)}, bf16[1,256,512]{2,1,0:T(8,128)(2,1)S(1)}, u32[]{:S(2)}, u32[]{:S(2)}) collective-permute-start(bf16[1,256,512]{2,1,0:T(8,128)(2,1)S(1)} %slice.50), channel_id=1, source_target_pairs={{4,0},{8,4},{12,8},{16,12},{20,16},{24,20},{28,24},{5,1},{9,5},{13... | collective-permute-start | bytes 786440 | tf_op jit(solution)/shard_map/ppermute | solution.py:21
  197.8 156.9 %copy-start.7 = (f32[128,128]{1,0:T(8,128)S(1)}, f32[128,128]{1,0:T(8,128)}, u32[]{:S(2)}) copy-start(f32[128,128]{1,0:T(8,128)} %param.33) | copy-start | bytes 196612
  197.8 156.9 %copy-start.12 = (f32[128,128]{1,0:T(8,128)S(1)}, f32[128,128]{1,0:T(8,128)}, u32[]{:S(2)}) copy-start(f32[128,128]{1,0:T(8,128)} %param.35) | copy-start | bytes 196612
  197.8 156.9 %copy-start.13 = (f32[128,128]{1,0:T(8,128)S(1)}, f32[128,128]{1,0:T(8,128)}, u32[]{:S(2)}) copy-start(f32[128,128]{1,0:T(8,128)} %param.34) | copy-start | bytes 196612
  197.8 157.6 %copy-start.11 = (f32[28,128]{1,0:T(8,128)S(1)}, f32[28,128]{1,0:T(8,128)}, u32[]{:S(2)}) copy-start(f32[28,128]{1,0:T(8,128)} %param.30) | copy-start | bytes 43012
  197.8 157.6 %copy-start.17 = (f32[28,128]{1,0:T(8,128)S(1)}, f32[28,128]{1,0:T(8,128)}, u32[]{:S(2)}) copy-start(f32[28,128]{1,0:T(8,128)} %param.32) | copy-start | bytes 43012
  197.8 157.6 %copy-start.18 = (f32[28,128]{1,0:T(8,128)S(1)}, f32[28,128]{1,0:T(8,128)}, u32[]{:S(2)}) copy-start(f32[28,128]{1,0:T(8,128)} %param.31) | copy-start | bytes 43012
  197.8 159.0 %copy-start.15 = (f32[20,128]{1,0:T(8,128)S(1)}, f32[20,128]{1,0:T(8,128)}, u32[]{:S(2)}) copy-start(f32[20,128]{1,0:T(8,128)} %param.27) | copy-start | bytes 30724
  197.8 159.0 %copy-start.20 = (f32[20,128]{1,0:T(8,128)S(1)}, f32[20,128]{1,0:T(8,128)}, u32[]{:S(2)}) copy-start(f32[20,128]{1,0:T(8,128)} %param.29) | copy-start | bytes 30724
  197.8 159.0 %copy-start.21 = (f32[20,128]{1,0:T(8,128)S(1)}, f32[20,128]{1,0:T(8,128)}, u32[]{:S(2)}) copy-start(f32[20,128]{1,0:T(8,128)} %param.28) | copy-start | bytes 30724
  197.8 160.4 %copy-start.6 = (f32[256,128]{1,0:T(8,128)S(1)}, f32[256,128]{1,0:T(8,128)}, u32[]{:S(2)}) copy-start(f32[256,128]{1,0:T(8,128)} %param.24) | copy-start | bytes 393220
  197.8 160.4 %copy-start.8 = (f32[256,128]{1,0:T(8,128)S(1)}, f32[256,128]{1,0:T(8,128)}, u32[]{:S(2)}) copy-start(f32[256,128]{1,0:T(8,128)} %param.26) | copy-start | bytes 393220
  197.8 160.4 %copy-start.9 = (f32[256,128]{1,0:T(8,128)S(1)}, f32[256,128]{1,0:T(8,128)}, u32[]{:S(2)}) copy-start(f32[256,128]{1,0:T(8,128)} %param.25) | copy-start | bytes 393220
  (13 other events, 75.3 us)
Sparse Core Ops, SparseCore 0:
  24.7 29.7 all-gather.4
  56.4 23.8 all-gather.6
  176.7 166.6 all-reduce.2
where the time goes:
time: 375 us; the launch traced here: 368 us
  waiting for transfers between devices  146 us (39%)
  matrix products  91.7 us (24%)
  blocking collectives  76.1 us (20%)
  other arithmetic  21.6 us (6%)
  between operations  18.4 us (5%)
  local copies, waits for them, and re-layouts  11.3 us (3%)
    psum x1, waiting for transfers between devices, on_device(): lax.psum((conv_grad, cond_grad, table_grad, out_grad), ('tm', 'batch'))  146 us
    dot_general x3, matrix products, contract_cols(): lax.dot_general(left, right, (((1,), (1,)), ((), ())), preferred_element_...  22 us
    dot_general x1, matrix products, on_device(): jnp.dot(flat_prev, conv_full[:channels], preferred_element_type=jnp.float32)  20 us
    all_gather x1, blocking collectives, on_device(): lax.all_gather(conv_weight.astype(jnp.bfloat16), 'batch', axis=0, tiled=T...  16.3 us
    all_gather x1, blocking collectives, on_device(): lax.all_gather(out_weight.astype(jnp.bfloat16), 'batch', axis=0, tiled=True)  14.5 us
    dot_general x3, matrix products, contract_rows(): lax.dot_general(left, right, (((0,), (0,)), ((), ())), preferred_element_...  14.1 us
    all_gather x1, blocking collectives, on_device(): lax.all_gather(cond_weight.astype(jnp.bfloat16), 'batch', axis=0, tiled=T...  13.1 us
    all_gather x1, blocking collectives, on_device(): lax.all_gather(speaker_table.astype(jnp.bfloat16), 'batch', axis=0, tiled...  13.1 us
  transfers between devices with their start and end apart: 5, of which 1 were waited for; matrix products, arithmetic and copies ran while one was open for 19% of the time, Pallas kernels for 0%

commit v1 on v0

--- a/solution.py
+++ b/solution.py
@@ -1,6 +1,10 @@
+import functools
+
 import jax
 import jax.numpy as jnp
 from jax import lax
+from jax.experimental import pallas as pl
+from jax.experimental.pallas import tpu as pltpu
 from jax.sharding import PartitionSpec as P
 
 DILATION_SIZE = 256
@@ -14,33 +18,22 @@
 decay_rate = 0.01
 learn_rate = 0.1
 
-
-def passed_along(value, axis, steps):
-    count = lax.axis_size(axis)
-    first, last = (max(0, -steps), min(count, count - steps))
-    return lax.ppermute(value, axis, [(source, source + steps) for source in range(first, last)])
-
-
-def contract_rows(left, right):
-    return lax.dot_general(
-        left, right, (((0,), (0,)), ((), ())), preferred_element_type=jnp.float32
-    )
-
-
-def contract_cols(left, right):
-    return lax.dot_general(
-        left, right, (((1,), (1,)), ((), ())), preferred_element_type=jnp.float32
-    )
-
-
-def own_block(whole, shard):
-    row_start = lax.axis_index("batch") * shard.shape[0]
-    col_start = lax.axis_index("tm") * shard.shape[1]
-    return lax.dynamic_slice(whole, (row_start, col_start), shard.shape)
-
-
-def square_sum(matrix):
-    return jnp.sum(matrix * matrix)
+LANES = 128
+MESH = pl.DeviceIdType.MESH
+BF16 = jnp.bfloat16
+F32 = jnp.float32
+
+
+def dot_nn(left, right):
+    return lax.dot_general(left, right, (((1,), (0,)), ((), ())), preferred_element_type=F32)
+
+
+def dot_nt(left, right):
+    return lax.dot_general(left, right, (((1,), (1,)), ((), ())), preferred_element_type=F32)
+
+
+def dot_tn(left, right):
+    return lax.dot_general(left, right, (((0,), (0,)), ((), ())), preferred_element_type=F32)
 
 
 def adamw(gradient, factor, master, first_old, second_old):
@@ -54,6 +47,808 @@
     )
     new_master = master - learn_rate * (step_size + decay_rate * master)
     return (new_first, new_second, new_master)
+
+
+class Layer:
+    def __init__(self, steps, channels, cond_dim, cond_rows, table_rows, seg_count):
+        self.steps = steps
+        self.channels = channels
+        self.cond_dim = cond_dim
+        self.cond_rows = cond_rows
+        self.table_rows = table_rows
+        self.seg_count = seg_count
+        self.misc_rows = 64
+        self.table_at = 32
+
+    CHUNKS = ((0, 128), (512, 128), (1024, 64), (1280, 128))
+    GRAD_ROWS = 1792
+
+    def scratch(self):
+        steps, ch = self.steps, self.channels
+        wide = 2 * ch
+        rows = self.GRAD_ROWS
+        dma = pltpu.SemaphoreType.DMA
+        return dict(
+            ax=pltpu.VMEM((steps + DILATION_SIZE, ch), BF16),
+            mp=pltpu.VMEM((steps, wide), F32),
+            gg=pltpu.VMEM((steps, ch), F32),
+            gated=pltpu.VMEM((steps, ch), BF16),
+            mg=pltpu.VMEM((steps, wide), BF16),
+            et=pltpu.VMEM((4 * self.misc_rows, steps), BF16),
+            cn=pltpu.VMEM((self.cond_dim, steps), BF16),
+            km=pltpu.VMEM((steps, LANES), F32),
+            wb=pltpu.VMEM((4, 2, 128, wide), BF16),
+            wo=pltpu.VMEM((4, 128, wide), BF16),
+            wm=pltpu.VMEM((4, self.misc_rows, wide), BF16),
+            conv_in=pltpu.VMEM((256, LANES), F32),
+            out_in=pltpu.VMEM((128, LANES), F32),
+            cond_in=pltpu.VMEM((self.cond_rows, LANES), F32),
+            table_in=pltpu.VMEM((self.table_rows, LANES), F32),
+            ss=pltpu.VMEM((rows, 4 * LANES), BF16),
+            sr=pltpu.VMEM((rows, 4 * LANES), BF16),
+            r1s=pltpu.VMEM((2, rows // 2, LANES), BF16),
+            r1r=pltpu.VMEM((2, rows // 2, LANES), BF16),
+            r3s=pltpu.VMEM((2, rows, LANES), BF16),
+            r3r=pltpu.VMEM((2, rows, LANES), BF16),
+            zs=pltpu.VMEM((rows, LANES), BF16),
+            zr=pltpu.VMEM((3, rows // 4, LANES), BF16),
+            phs=pltpu.VMEM((DILATION_SIZE, ch), BF16),
+            phr=pltpu.VMEM((DILATION_SIZE, ch), BF16),
+            nplane=pltpu.VMEM((8, 8, LANES), F32),
+            nline=pltpu.VMEM((4, 8, LANES), F32),
+            g_send=dma((4, 11)),
+            g_recv=dma((4, 11)),
+            r_send=dma((4, 8)),
+            r_recv=dma((4, 8)),
+            n_send=dma((10,)),
+            n_recv=dma((10,)),
+            h_send=dma((2,)),
+            h_recv=dma((2,)),
+            local=dma((8,)),
+        )
+
+    def kernel(
+        self, ids, starts, audio, conditioning, grad_res, grad_skip, conv_w, cond_w, table_w, out_w, *rest
+    ):
+        names = list(self.scratch())
+        outs, bufs = rest[: len(rest) - len(names)], rest[len(rest) - len(names) :]
+        res, skip, agrad, fconv, fmisc, fout, norm = outs
+        b = dict(zip(names, bufs))
+        steps, ch = self.steps, self.channels
+        ax, mp, gg, gated, mg = b["ax"], b["mp"], b["gg"], b["gated"], b["mg"]
+        et, cn, km, wb, wo, wm = b["et"], b["cn"], b["km"], b["wb"], b["wo"], b["wm"]
+        pv = res
+
+        t = lax.axis_index("tm")
+        z = lax.axis_index("batch")
+        core = lax.rem(t, 2)
+        chip = t // 2
+        sib = t + 1 - 2 * core
+        xbit = lax.rem(chip, 2)
+        ybit = chip // 2
+        xdelta = 1 - 2 * xbit
+        ydelta = 2 * (1 - 2 * ybit)
+        chip_x, chip_y, chip_d = chip + xdelta, chip + ydelta, chip + xdelta + ydelta
+        tx, ty, td = 2 * chip_x + core, 2 * chip_y + core, 2 * chip_d + core
+        zlow, zhigh = lax.rem(z, 2), z // 2
+        zdelta = (1 - 2 * zlow, 2 * (1 - 2 * zhigh))
+        zpeers = (z + zdelta[0], z + zdelta[1], z + zdelta[0] + zdelta[1])
+        tlow, tmid, thigh = core, xbit, ybit
+
+        def lanes(block):
+            return pl.ds(pl.multiple_of(block * LANES, LANES), LANES)
+
+        def rows_at(start, size):
+            return pl.ds(pl.multiple_of(start, 16), size)
+
+        def local(i, source, target):
+            return pltpu.make_async_copy(source, target, b["local"].at[i])
+
+        small = [
+            local(0, conv_w, b["conv_in"]),
+            local(1, out_w, b["out_in"]),
+            local(2, cond_w, b["cond_in"]),
+            local(3, table_w, b["table_in"]),
+        ]
+        own_ax = ax.at[pl.ds(DILATION_SIZE, steps), :]
+        large = [
+            local(4, audio.at[0], own_ax),
+            local(5, conditioning.at[0], cn),
+            local(6, grad_res.at[0], agrad),
+            local(7, grad_skip.at[0], skip),
+        ]
+        for copy in small:
+            copy.start()
+
+        barrier = pltpu.get_barrier_semaphore()
+        plane = []
+        for k in range(1, 8):
+            dt = (
+                (1 - 2 * tlow) * (k & 1)
+                + 2 * (1 - 2 * tmid) * ((k >> 1) & 1)
+                + 4 * (1 - 2 * thigh) * ((k >> 2) & 1)
+            )
+            plane.append(t + dt)
+        for peer in plane:
+            pl.semaphore_signal(barrier, inc=1, device_id=(peer, z), device_id_type=MESH)
+        for peer in zpeers:
+            pl.semaphore_signal(barrier, inc=1, device_id=(t, peer), device_id_type=MESH)
+        for copy in large:
+            copy.start()
+
+        for copy in small:
+            copy.wait()
+        for h in range(2):
+            wb[z, h, :, lanes(t)] = b["conv_in"][h * 128 : (h + 1) * 128, :].astype(BF16)
+        wo[z, :, lanes(t)] = b["out_in"][...].astype(BF16)
+        pad_c = jnp.zeros((self.table_at - self.cond_rows, LANES), F32)
+        pad_t = jnp.zeros((self.misc_rows - self.table_at - self.table_rows, LANES), F32)
+        wm[z, :, lanes(t)] = jnp.concatenate(
+            [b["cond_in"][...], pad_c, b["table_in"][...], pad_t], axis=0
+        ).astype(BF16)
+        pl.semaphore_wait(barrier, 10)
+
+        def part(chunk, block, zs=None):
+            whole = zs is None
+            if chunk == 0:
+                return wo.at[:, :, lanes(block)] if whole else wo.at[zs, :, lanes(block)]
+            if chunk == 1:
+                return wm.at[:, :, lanes(block)] if whole else wm.at[zs, :, lanes(block)]
+            h = chunk - 2
+            return wb.at[:, h, :, lanes(block)] if whole else wb.at[zs, h, :, lanes(block)]
+
+        def push(ref, i, chunk, where):
+            return pltpu.make_async_remote_copy(
+                src_ref=ref,
+                dst_ref=ref,
+                send_sem=b["g_send"].at[chunk, i],
+                recv_sem=b["g_recv"].at[chunk, i],
+                device_id=where,
+                device_id_type=MESH,
+            )
+
+        def g_copy(chunk, i):
+            if i < 3:
+                return push(part(chunk, t, pl.ds(z, 1)), i, chunk, (t, zpeers[i]))
+            if i == 3:
+                return push(part(chunk, t), i, chunk, (tx, z))
+            if i == 4:
+                return push(part(chunk, t), i, chunk, (ty, z))
+            if i == 5:
+                return push(part(chunk, tx, pl.ds(0, 2)), i, chunk, (ty, z))
+            if i == 6:
+                return push(part(chunk, ty, pl.ds(2, 2)), i, chunk, (tx, z))
+            block = (t, tx, ty, td)[i - 7] if i < 11 else None
+            return push(part(chunk, block), i, chunk, (sib, z))
+
+        def g_start(chunk, i):
+            g_copy(chunk, i).start()
+
+        def g_wait(chunk, i):
+            g_copy(chunk, i).wait_recv()
+
+        def g_z(chunk):
+            for i in range(3):
+                g_start(chunk, i)
+
+        def g_xy(chunk):
+            for i in range(3):
+                g_wait(chunk, i)
+            for i in (3, 4, 7):
+                g_start(chunk, i)
+
+        def g_f(chunk):
+            g_wait(chunk, 3)
+            g_start(chunk, 5)
+            g_start(chunk, 8)
+            g_wait(chunk, 4)
+            g_start(chunk, 6)
+            g_start(chunk, 9)
+
+        def g_d(chunk):
+            g_wait(chunk, 5)
+            g_wait(chunk, 6)
+            g_start(chunk, 10)
+
+        def g_s(chunk):
+            for i in range(7, 11):
+                g_wait(chunk, i)
+
+        def halo_in():
+            return pltpu.make_async_remote_copy(
+                src_ref=audio.at[0, pl.ds(steps - DILATION_SIZE, DILATION_SIZE), :],
+                dst_ref=ax.at[pl.ds(0, DILATION_SIZE), :],
+                send_sem=b["h_send"].at[0],
+                recv_sem=b["h_recv"].at[0],
+                device_id=(jnp.minimum(t + 1, 7), z),
+                device_id_type=MESH,
+            )
+
+        def halo_back():
+            return pltpu.make_async_remote_copy(
+                src_ref=b["phs"],
+                dst_ref=b["phr"],
+                send_sem=b["h_send"].at[1],
+                recv_sem=b["h_recv"].at[1],
+                device_id=(jnp.maximum(t - 1, 0), z),
+                device_id_type=MESH,
+            )
+
+        def loop(count, body):
+            lax.fori_loop(0, count, lambda i, c: (body(i), c)[1], 0)
+
+        def make_mask():
+            size = 256
+
+            def body(i):
+                at = rows_at(i * size, size)
+                p = (
+                    t * steps
+                    + i * size
+                    + lax.broadcasted_iota(jnp.int32, (size, LANES), 0)
+                )
+                drop = None
+                for j in range(self.seg_count):
+                    d = p - starts[0, j]
+                    hit = (d >= 0) & (d < DILATION_SIZE)
+                    drop = hit if drop is None else drop | hit
+                km[at, :] = jnp.where(drop, 0.0, 1.0)
+
+            loop(steps // size, body)
+
+        def make_extra():
+            cut = 1024
+            n = self.misc_rows
+            for c in range(steps // cut):
+                at = pl.ds(c * cut, cut)
+                p = t * steps + c * cut + lax.broadcasted_iota(jnp.int32, (1, cut), 1)
+                speaker = jnp.full((1, cut), ids[0, 0], jnp.int32)
+                for j in range(1, self.seg_count):
+                    speaker = jnp.where(p >= starts[0, j], ids[0, j], speaker)
+                wide_speaker = jnp.broadcast_to(speaker, (n, cut))
+                for q in range(4):
+                    row = lax.broadcasted_iota(jnp.int32, (n, self.cond_dim), 0)
+                    col = lax.broadcasted_iota(jnp.int32, (n, self.cond_dim), 1)
+                    pick = (col == row + q * self.cond_rows) & (row < self.cond_rows)
+                    pick = jnp.where(pick, 1.0, 0.0).astype(BF16)
+                    mel = dot_nn(pick, cn[:, at])
+                    slot = lax.broadcasted_iota(jnp.int32, (n, cut), 0) - self.table_at
+                    ours = (slot >= 0) & (slot < self.table_rows)
+                    hot = ours & (slot + q * self.table_rows == wide_speaker)
+                    et[q * n : (q + 1) * n, at] = jnp.where(hot, 1.0, mel).astype(BF16)
+
+        def make_prev():
+            size = 512
+
+            def body(i):
+                at = rows_at(i * size, size)
+                keep = km[at, :].astype(BF16)
+                pv[at, :] = ax[at, :] * jnp.concatenate([keep] * (ch // LANES), axis=1)
+
+            loop(steps // size, body)
+
+        def gated_grad():
+            size = 1024
+
+            def body(i):
+                at = rows_at(i * size, size)
+                w = wo[...].reshape(ch, 2 * ch)
+                gg[at, :] = dot_nt(agrad[at, :], w[:, :ch]) + dot_nt(skip[at, :], w[:, ch:])
+
+            loop(steps // size, body)
+
+        def taps(i, size, h):
+            at = rows_at(i * size, size)
+            cur = pl.ds(pl.multiple_of(i * size + DILATION_SIZE, DILATION_SIZE), size)
+            lo = slice(h * 128, h * 128 + 128)
+            hi = slice(256 + h * 128, 256 + h * 128 + 128)
+            return jnp.concatenate([pv[at, lo], pv[at, hi], ax[cur, lo], ax[cur, hi]], axis=1)
+
+        def mixture_first():
+            size = 1024
+
+            def body(i):
+                at = rows_at(i * size, size)
+                lhs = taps(i, size, 0)
+                cut = pl.ds(pl.multiple_of(i * size, size), size)
+                for n in range(4):
+                    cols = slice(n * 256, (n + 1) * 256)
+                    w = wb[:, 0, :, cols].reshape(512, 256)
+                    m = wm[:, :, cols].reshape(4 * self.misc_rows, 256)
+                    mp[at, cols] = dot_nn(lhs, w) + dot_tn(et[:, cut], m)
+
+            loop(steps // size, body)
+
+        def gate():
+            size = 1024
+
+            def body(i):
+                at = rows_at(i * size, size)
+                lhs = taps(i, size, 1)
+                for n in range(ch // 256):
+                    c0 = slice(n * 256, (n + 1) * 256)
+                    c1 = slice(ch + n * 256, ch + (n + 1) * 256)
+                    x = mp[at, c0] + dot_nn(lhs, wb[:, 1, :, c0].reshape(512, 256))
+                    y = mp[at, c1] + dot_nn(lhs, wb[:, 1, :, c1].reshape(512, 256))
+                    th = jnp.tanh(x)
+                    sg = 0.5 * jnp.tanh(0.5 * y) + 0.5
+                    q = gg[at, c0]
+                    g = th * sg
+                    gated[at, c0] = g.astype(BF16)
+                    mg[at, c0] = (q * (sg - g * th)).astype(BF16)
+                    mg[at, c1] = (q * (g - g * sg)).astype(BF16)
+
+            loop(steps // size, body)
+
+        def wtaps(first):
+            return wb[first : first + 2].reshape(ch, 2 * ch)
+
+        def head_back():
+            at = pl.ds(0, DILATION_SIZE)
+            keep = jnp.concatenate([km[at, :]] * (ch // LANES), axis=1)
+            b["phs"][...] = (keep * dot_nt(mg[at, :], wtaps(0))).astype(BF16)
+
+            @pl.when(t > 0)
+            def _():
+                halo_back().start()
+
+        def store_grad(row, value):
+            size = value.shape[0]
+            at = pl.ds(row, size)
+            even = core == 0
+            for k in range(4):
+                left = value[:, 2 * k * LANES : (2 * k + 1) * LANES]
+                right = value[:, (2 * k + 1) * LANES : (2 * k + 2) * LANES]
+                cols = slice(k * LANES, (k + 1) * LANES)
+                mp[at, cols] = jnp.where(even, left, right)
+                b["ss"][at, cols] = jnp.where(even, right, left).astype(BF16)
+
+        def conv_grad(h, side):
+            lo = slice(h * 128, h * 128 + 128)
+            hi = slice(256 + h * 128, 256 + h * 128 + 128)
+            if side == 0:
+                lhs = jnp.concatenate([pv[:, lo], pv[:, hi]], axis=1)
+            else:
+                cur = pl.ds(DILATION_SIZE, steps)
+                lhs = jnp.concatenate([ax[cur, lo], ax[cur, hi]], axis=1)
+            store_grad(512 * h + 256 * side, dot_tn(lhs, mg[...]))
+
+        def misc_grad():
+            store_grad(1024, dot_nn(et[...], mg[...]))
+
+        def out_grad(side):
+            lhs = gated[:, side * 256 : (side + 1) * 256]
+            value = jnp.concatenate([dot_tn(lhs, agrad[...]), dot_tn(lhs, skip[...])], axis=1)
+            store_grad(1280 + 256 * side, value)
+
+        def projected(which):
+            size = 1024
+
+            def body(i):
+                at = rows_at(i * size, size)
+                if which == 0:
+                    w = wo[:, :, :ch].reshape(ch, ch)
+                    cur = pl.ds(pl.multiple_of(i * size + DILATION_SIZE, DILATION_SIZE), size)
+                    res[at, :] = (ax[cur, :].astype(F32) + dot_nn(gated[at, :], w)).astype(BF16)
+                else:
+                    w = wo[:, :, ch:].reshape(ch, ch)
+                    skip[at, :] = dot_nn(gated[at, :], w).astype(BF16)
+
+            loop(steps // size, body)
+
+        def audio_block(at, later):
+            keep = jnp.concatenate([km[later, :]] * (ch // LANES), axis=1)
+            total = agrad[at, :].astype(F32) + dot_nt(mg[at, :], wtaps(2))
+            agrad[at, :] = (total + keep * dot_nt(mg[later, :], wtaps(0))).astype(BF16)
+
+        def audio_main():
+            def body(i):
+                at = rows_at(i * 1024, 1024)
+                later = pl.ds(pl.multiple_of(i * 1024 + DILATION_SIZE, DILATION_SIZE), 1024)
+                audio_block(at, later)
+
+            loop(2, body)
+
+        def audio_rest():
+            size = steps - 2048 - DILATION_SIZE
+            audio_block(pl.ds(2048, size), pl.ds(2048 + DILATION_SIZE, size))
+
+        def audio_last():
+            @pl.when(t < 7)
+            def _():
+                halo_back().wait_recv()
+
+            @pl.when(t == 7)
+            def _():
+                b["phr"][...] = jnp.zeros((DILATION_SIZE, ch), BF16)
+
+            at = pl.ds(steps - DILATION_SIZE, DILATION_SIZE)
+            total = agrad[at, :].astype(F32) + dot_nt(mg[at, :], wtaps(2))
+            agrad[at, :] = (total + b["phr"][...].astype(F32)).astype(BF16)
+
+        def r_copy(j, i):
+            row, r = self.CHUNKS[j]
+            if i == 0:
+                at = pl.ds(row, 4 * r)
+                source, target, where = b["ss"].at[at, :], b["sr"].at[at, :], (sib, z)
+            elif i < 3:
+                at = pl.ds(row // 2, 2 * r)
+                source, target = b["r1s"].at[i - 1, at, :], b["r1r"].at[i - 1, at, :]
+                where = (tx, z) if i == 1 else (ty, z)
+            elif i < 5:
+                at = pl.ds(row, 4 * r)
+                source, target = b["r3s"].at[i - 3, at, :], b["r3r"].at[i - 3, at, :]
+                where = (tx, z) if i == 3 else (ty, z)
+            else:
+                peer = zpeers[i - 5]
+                source = b["zs"].at[rows_at(row + peer * r, r), :]
+                target = b["zr"].at[i - 5, pl.ds(row // 4, r), :]
+                where = (t, peer)
+            return pltpu.make_async_remote_copy(
+                src_ref=source,
+                dst_ref=target,
+                send_sem=b["r_send"].at[j, i],
+                recv_sem=b["r_recv"].at[j, i],
+                device_id=where,
+                device_id_type=MESH,
+            )
+
+        def pair_sum(at, block):
+            return mp[at, lanes(block)] + b["sr"][at, lanes(block)].astype(F32)
+
+        def r_s(j):
+            r_copy(j, 0).start()
+
+        def r_1(j):
+            row, r = self.CHUNKS[j]
+            r_copy(j, 0).wait_recv()
+            half = pl.ds(row // 2, 2 * r)
+            b["r1s"][0, half, :] = pair_sum(pl.ds(row, 2 * r), chip_d).astype(BF16)
+            r_copy(j, 1).start()
+            b["r1s"][1, half, :] = pair_sum(pl.ds(row + 2 * r, 2 * r), chip_d).astype(BF16)
+            r_copy(j, 2).start()
+
+        def r_3(j):
+            row, r = self.CHUNKS[j]
+            up, low = pl.ds(row, 2 * r), pl.ds(row + 2 * r, 2 * r)
+            half = pl.ds(row // 2, 2 * r)
+            b["r3s"][0, up, :] = pair_sum(up, chip_x).astype(BF16)
+            b["r3s"][1, low, :] = pair_sum(low, chip_y).astype(BF16)
+            r_copy(j, 2).wait_recv()
+            b["r3s"][0, low, :] = (
+                pair_sum(low, chip_x) + b["r1r"][1, half, :].astype(F32)
+            ).astype(BF16)
+            r_copy(j, 3).start()
+            r_copy(j, 1).wait_recv()
+            b["r3s"][1, up, :] = (
+                pair_sum(up, chip_y) + b["r1r"][0, half, :].astype(F32)
+            ).astype(BF16)
+            r_copy(j, 4).start()
+
+        def plane_sum(at):
+            return (
+                pair_sum(at, chip)
+                + b["r3r"][0, at, :].astype(F32)
+                + b["r3r"][1, at, :].astype(F32)
+            )
+
+        def final(j):
+            return (fconv.at[pl.ds(0, 128), :], fconv.at[pl.ds(128, 128), :], fmisc, fout)[j]
+
+        def r_z(j):
+            row, r = self.CHUNKS[j]
+            r_copy(j, 3).wait_recv()
+            r_copy(j, 4).wait_recv()
+            at = pl.ds(row, 4 * r)
+            b["zs"][at, :] = plane_sum(at).astype(BF16)
+            for i in range(5, 8):
+                r_copy(j, i).start()
+            final(j)[...] = plane_sum(rows_at(row + z * r, r))
+
+        def r_f(j):
+            row, r = self.CHUNKS[j]
+            total = final(j)[...]
+            for i in range(5, 8):
+                r_copy(j, i).wait_recv()
+                total = total + b["zr"][i - 5, pl.ds(row // 4, r), :].astype(F32)
+            final(j)[...] = total
+
+        def tile_squares():
+            total = jnp.zeros((8, LANES), F32)
+            for j in range(4):
+                value = final(j)[...]
+                total = total + jnp.sum((value * value).reshape(-1, 8, LANES), axis=0)
+            return total
+
+        def n_copy(i):
+            if i < 7:
+                ref, where = b["nplane"].at[t], (plane[i], z)
+            else:
+                ref, where = b["nline"].at[z], (t, zpeers[i - 7])
+            return pltpu.make_async_remote_copy(
+                src_ref=ref,
+                dst_ref=ref,
+                send_sem=b["n_send"].at[i],
+                recv_sem=b["n_recv"].at[i],
+                device_id=where,
+                device_id_type=MESH,
+            )
+
+        def norm_plane():
+            b["nplane"][t] = tile_squares()
+            for i in range(7):
+                n_copy(i).start()
+
+        def norm_line():
+            for i in range(7):
+                n_copy(i).wait_recv()
+            total = b["nplane"][0]
+            for k in range(1, 8):
+                total = total + b["nplane"][k]
+            b["nline"][z] = total
+            for i in range(7, 10):
+                n_copy(i).start()
+
+        def norm_end():
+            for i in range(7, 10):
+                n_copy(i).wait_recv()
+            total = b["nline"][0]
+            for k in range(1, 4):
+                total = total + b["nline"][k]
+            norm[...] = total
+
+        for chunk in (0, 1, 2, 3):
+            g_z(chunk)
+
+        @pl.when(t < 7)
+        def _():
+            halo_in().start()
+
+        make_mask()
+        large[1].wait()
+        make_extra()
+        large[0].wait()
+
+        @pl.when(t == 0)
+        def _():
+            ax[pl.ds(0, DILATION_SIZE), :] = jnp.zeros((DILATION_SIZE, ch), BF16)
+
+        g_xy(0)
+        g_xy(1)
+        g_xy(2)
+        g_f(0)
+
+        @pl.when(t > 0)
+        def _():
+            halo_in().wait_recv()
+
+        make_prev()
+        g_xy(3)
+        g_f(1)
+        g_d(0)
+        g_f(2)
+        large[2].wait()
+        large[3].wait()
+        g_s(0)
+        gated_grad()
+        g_f(3)
+        g_d(1)
+        g_d(2)
+        g_s(1)
+        g_s(2)
+        mixture_first()
+        g_d(3)
+        g_s(3)
+        gate()
+        head_back()
+        conv_grad(0, 0)
+        conv_grad(0, 1)
+        r_s(0)
+        conv_grad(1, 0)
+        r_1(0)
+        conv_grad(1, 1)
+        r_s(1)
+        r_3(0)
+        misc_grad()
+        r_s(2)
+        r_1(1)
+        out_grad(0)
+        r_z(0)
+        r_3(1)
+        r_1(2)
+        out_grad(1)
+        r_s(3)
+        r_3(2)
+        audio_main()
+        r_1(3)
+        r_z(1)
+        r_z(2)
+        r_f(0)
+        audio_rest()
+        r_3(3)
+        audio_last()
+        r_f(1)
+        projected(0)
+        r_z(3)
+        r_f(2)
+        projected(1)
+        r_f(3)
+        norm_plane()
+        norm_line()
+        norm_end()
+
+        for chunk in range(4):
+            for i in range(11):
+                g_copy(chunk, i).wait_send()
+        for j in range(4):
+            for i in range(8):
+                r_copy(j, i).wait_send()
+        for i in range(10):
+            n_copy(i).wait_send()
+
+        @pl.when(t < 7)
+        def _():
+            halo_in().wait_send()
+
+        @pl.when(t > 0)
+        def _():
+            halo_back().wait_send()
+
+    def __call__(self, ids, starts, audio, conditioning, grad_res, grad_skip, conv_w, cond_w, table_w, out_w):
+        steps, ch = self.steps, self.channels
+        wide = pltpu.VMEM((steps, ch), BF16)
+        smem = pl.BlockSpec(memory_space=pltpu.SMEM)
+        anywhere = pl.BlockSpec(memory_space=pl.ANY)
+        vmem = pl.BlockSpec(memory_space=pltpu.VMEM)
+        return pl.pallas_call(
+            self.kernel,
+            out_shape=[
+                wide,
+                wide,
+                wide,
+                pltpu.VMEM((256, LANES), F32),
+                pltpu.VMEM((self.misc_rows, LANES), F32),
+                pltpu.VMEM((128, LANES), F32),
+                pltpu.VMEM((8, LANES), F32),
+            ],
+            in_specs=[smem, smem] + [anywhere] * 8,
+            out_specs=[vmem] * 7,
+            scratch_shapes=list(self.scratch().values()),
+            compiler_params=pltpu.CompilerParams(
+                collective_id=0, has_side_effects=True, vmem_limit_bytes=52 * 2**20
+            ),
+            name="layer",
+        )(ids, starts, audio, conditioning, grad_res, grad_skip, conv_w, cond_w, table_w, out_w)
+
+
+def closing_kernel(cond_rows, table_at, table_rows, *refs):
+    (res, skip, agrad, fconv, fmisc, fout, norm), refs = refs[:7], refs[7:]
+    state, refs = refs[:12], refs[12:]
+    (res_o, skip_o, agrad_o, prenorm_o), refs = refs[:4], refs[4:]
+    new, (sems,) = refs[:12], refs[12:]
+    copies = [
+        pltpu.make_async_copy(source, target.at[0], sems.at[i])
+        for i, (source, target) in enumerate(((res, res_o), (skip, skip_o), (agrad, agrad_o)))
+    ]
+    for copy in copies:
+        copy.start()
+    prenorm = jnp.sqrt(jnp.sum(norm[...], keepdims=True))
+    prenorm_o[...] = prenorm
+    factor = jnp.minimum(1.0, clip_level / (prenorm + 1e-06))
+    grads = (
+        fconv[...],
+        fmisc[0:cond_rows, :],
+        fmisc[table_at : table_at + table_rows, :],
+        fout[...],
+    )
+    for k, grad in enumerate(grads):
+        master, first, second = (state[3 * k + i][...] for i in range(3))
+        for i, value in enumerate(adamw(grad, factor, master, first, second)):
+            new[3 * k + i][...] = value
+    for copy in copies:
+        copy.wait()
+
+
+def closing(layer, results, state):
+    wide = jax.ShapeDtypeStruct((1, layer.steps, layer.channels), BF16)
+    vmem = pl.BlockSpec(memory_space=pltpu.VMEM)
+    anywhere = pl.BlockSpec(memory_space=pl.ANY)
+    return pl.pallas_call(
+        functools.partial(closing_kernel, layer.cond_rows, layer.table_at, layer.table_rows),
+        out_shape=[wide, wide, wide, jax.ShapeDtypeStruct((1, 1), F32)]
+        + [jax.ShapeDtypeStruct(a.shape, F32) for a in state],
+        in_specs=[vmem] * 19,
+        out_specs=[anywhere] * 3 + [vmem] * 13,
+        scratch_shapes=[pltpu.SemaphoreType.DMA((3,))],
+        compiler_params=pltpu.CompilerParams(vmem_limit_bytes=32 * 2**20),
+        name="closing",
+    )(*results, *state)
+
+
+def on_device_kernels(
+    audio,
+    conditioning,
+    speaker_ids,
+    seg_starts,
+    grad_residual,
+    grad_skip,
+    conv_weight,
+    conv_first,
+    conv_second,
+    cond_weight,
+    cond_first,
+    cond_second,
+    speaker_table,
+    table_first,
+    table_second,
+    out_weight,
+    out_first,
+    out_second,
+):
+    layer = Layer(
+        audio.shape[1],
+        audio.shape[2],
+        conditioning.shape[1],
+        cond_weight.shape[0],
+        speaker_table.shape[0],
+        seg_starts.shape[1],
+    )
+    results = layer(
+        speaker_ids,
+        seg_starts,
+        audio,
+        conditioning,
+        grad_residual,
+        grad_skip,
+        conv_weight,
+        cond_weight,
+        speaker_table,
+        out_weight,
+    )
+    state = (
+        conv_weight,
+        conv_first,
+        conv_second,
+        cond_weight,
+        cond_first,
+        cond_second,
+        speaker_table,
+        table_first,
+        table_second,
+        out_weight,
+        out_first,
+        out_second,
+    )
+    done = closing(layer, results, state)
+    return (done[0], done[1], done[2], done[3].reshape(()), *done[4:])
+
+
+def passed_along(value, axis, steps):
+    count = lax.axis_size(axis)
+    first, last = (max(0, -steps), min(count, count - steps))
+    return lax.ppermute(value, axis, [(source, source + steps) for source in range(first, last)])
+
+
+def contract_rows(left, right):
+    return lax.dot_general(
+        left, right, (((0,), (0,)), ((), ())), preferred_element_type=jnp.float32
+    )
+
+
+def contract_cols(left, right):
+    return lax.dot_general(
+        left, right, (((1,), (1,)), ((), ())), preferred_element_type=jnp.float32
+    )
+
+
+def own_block(whole, shard):
+    row_start = lax.axis_index("batch") * shard.shape[0]
+    col_start = lax.axis_index("tm") * shard.shape[1]
+    return lax.dynamic_slice(whole, (row_start, col_start), shard.shape)
+
+
+def square_sum(matrix):
+    return jnp.sum(matrix * matrix)
 
 
 def on_device(
@@ -229,8 +1024,9 @@
         P("batch", "tm"),
         P("batch", "tm"),
     )
+    small = mesh.shape["tm"] == 8 and mesh.shape["batch"] == 4
     return jax.shard_map(
-        on_device,
+        on_device_kernels if small else on_device,
         mesh=mesh,
         in_specs=placed,
         out_specs=(

time: 375 us -> 93.8 us (0.25); the launches traced: 368 us -> 93.7 us
  waiting for transfers between devices: 146 us -> 0 us
  Pallas kernels: 0 us -> 92.6 us
  matrix products: 91.7 us -> 0 us
  blocking collectives: 76.1 us -> 0 us
  other arithmetic: 21.6 us -> 0 us
  between operations: 18.4 us -> 1.03 us
  local copies, waits for them, and re-layouts: 11.3 us -> 0.05 us
    psum x1 -> x0, waiting for transfers between devices: 146 us -> none  [on_device(): lax.psum((conv_grad, cond_grad, table_grad, out_grad), ('tm', 'batch'))]
    pallas_call x0 -> x2, Pallas kernels: none -> 92.6 us  [the longest x1 87.9 us: __call__(): pl.pallas_call(self.kernel, out_shape=[wide, wide, wide, pltpu.VMEM((256,...]
    dot_general x14 -> x0, matrix products: 91.7 us -> none  [the longest x3 22 us: contract_cols(): lax.dot_general(left, right, (((1,), (1,)), ((), ())), preferred_element_...]
    all_gather x6 -> x0, blocking collectives: 76.1 us -> none  [the longest x1 16.3 us: on_device(): lax.all_gather(conv_weight.astype(jnp.bfloat16), 'batch', axis=0, tiled=T...]
    reduce_sum x6 -> x0, other arithmetic: 8.76 us -> none  [the longest x4 8.56 us: square_sum(): return jnp.sum(matrix * matrix)]
    sub x5 -> x0, other arithmetic: 5.31 us -> none  [the longest x4 5.31 us: adamw(): new_master = master - learn_rate * (step_size + decay_rate * master)]
    unnamed x64 -> x24, local copies, waits for them, and re-layouts: 4.58 us -> 0.05 us
  transfers between devices with their start and end apart: 5 -> 0, of which waited for: 1 -> 0; matrix products, arithmetic and copies ran while one was open for 19% -> 0% of each run, Pallas kernels for 0% -> 0%
where the time goes in v1:
time: 93.8 us; the launch traced here: 93.7 us
  Pallas kernels  92.6 us (99%)
  between operations  1.03 us (1%)
    pallas_call x1, Pallas kernels, __call__(): pl.pallas_call(self.kernel, out_shape=[wide, wide, wide, pltpu.VMEM((256,...  87.9 us
    pallas_call x1, Pallas kernels, closing(): pl.pallas_call(functools.partial(closing_kernel, layer.cond_rows, layer.t...  4.65 us

profile of v1, /device:TPU:0, one launch (start us, length us, event | category | flops | bytes accessed | tf_op | source)
XLA Modules:
  0.0 93.7 jit_solution(6970197689241532207)
XLA Ops:
  0.7 0.0 copy-start.1
  0.7 0.0 copy-start.6
  0.7 0.0 copy-start.7
  0.7 0.0 copy-start
  0.7 0.0 copy-start.5
  0.7 0.0 copy-start.4
  0.7 0.0 copy-start.9
  0.7 0.0 copy-start.8
  0.7 0.0 copy-start.11
  0.7 0.0 copy-start.10
  0.8 0.0 copy-start.3
  0.8 0.0 copy-start.2
  0.8 87.9 %layer.1 = (bf16[3072,512]{1,0:T(8,128)(2,1)S(1)}, bf16[3072,512]{1,0:T(8,128)(2,1)S(1)}, bf16[3072,512]{1,0:T(8,128)(2,1)S(1)}, f32[256,128]{1,0:T(8,128)S(1)},...) custom-call(s32[1,8]{1,0:T(1,128)} %ids.1, s32[1,8]{1,0:T(1,128)} %starts.1, ...), custom_call_target="tpu_custom_call" | custom-call | tf_op jit(solution)/shard_map/layer/pallas_call | solution.py:703
  88.7 0.0 copy-done.1
  88.7 0.0 copy-done.6
  88.7 0.0 copy-done.7
  88.8 0.0 copy-done
  88.8 0.0 copy-done.5
  88.8 0.0 copy-done.4
  88.8 0.0 copy-done.9
  88.8 0.0 copy-done.8
  88.8 0.0 copy-done.11
  88.8 0.0 copy-done.10
  88.8 4.6 %closing.1 = (bf16[1,3072,512]{2,1,0:T(8,128)(2,1)}, bf16[1,3072,512]{2,1,0:T(8,128)(2,1)}, bf16[1,3072,512]{2,1,0:T(8,128)(2,1)}, f32[1,1]{1,0:T(1,128)}, f32[2...) custom-call(bf16[3072,512]{1,0:T(8,128)(2,1)S(1)} %get-tuple-element, ...), custom_call_target="tpu_custom_call" | custom-call | tf_op jit(solution)/shard_map/closing/pallas_call | solution.py:756
  (2 shorter events, 0.0 us)
Async XLA Ops:
  0.7 88.1 %copy-start.1 = (f32[128,128]{1,0:T(8,128)S(1)}, f32[128,128]{1,0:T(8,128)}, u32[]{:S(2)}) copy-start(f32[128,128]{1,0:T(8,128)} %refs_16_.1) | copy-start | bytes 196612
  0.7 88.1 %copy-start.6 = (f32[28,128]{1,0:T(8,128)S(1)}, f32[28,128]{1,0:T(8,128)}, u32[]{:S(2)}) copy-start(f32[28,128]{1,0:T(8,128)} %refs_13_.1) | copy-start | bytes 43012
  0.7 88.1 %copy-start.7 = (f32[20,128]{1,0:T(8,128)S(1)}, f32[20,128]{1,0:T(8,128)}, u32[]{:S(2)}) copy-start(f32[20,128]{1,0:T(8,128)} %refs_10_.1) | copy-start | bytes 30724
  0.7 88.1 %copy-start = (f32[256,128]{1,0:T(8,128)S(1)}, f32[256,128]{1,0:T(8,128)}, u32[]{:S(2)}) copy-start(f32[256,128]{1,0:T(8,128)} %refs_7_.1) | copy-start | bytes 393220
  0.7 88.1 %copy-start.5 = (f32[128,128]{1,0:T(8,128)S(1)}, f32[128,128]{1,0:T(8,128)}, u32[]{:S(2)}) copy-start(f32[128,128]{1,0:T(8,128)} %refs_18_.1) | copy-start | bytes 196612
  0.7 88.1 %copy-start.4 = (f32[128,128]{1,0:T(8,128)S(1)}, f32[128,128]{1,0:T(8,128)}, u32[]{:S(2)}) copy-start(f32[128,128]{1,0:T(8,128)} %refs_17_.1) | copy-start | bytes 196612
  0.7 88.1 %copy-start.9 = (f32[28,128]{1,0:T(8,128)S(1)}, f32[28,128]{1,0:T(8,128)}, u32[]{:S(2)}) copy-start(f32[28,128]{1,0:T(8,128)} %refs_15_.1) | copy-start | bytes 43012
  0.7 88.1 %copy-start.8 = (f32[28,128]{1,0:T(8,128)S(1)}, f32[28,128]{1,0:T(8,128)}, u32[]{:S(2)}) copy-start(f32[28,128]{1,0:T(8,128)} %refs_14_.1) | copy-start | bytes 43012
  0.7 88.1 %copy-start.11 = (f32[20,128]{1,0:T(8,128)S(1)}, f32[20,128]{1,0:T(8,128)}, u32[]{:S(2)}) copy-start(f32[20,128]{1,0:T(8,128)} %refs_12_.1) | copy-start | bytes 30724
  0.7 88.1 %copy-start.10 = (f32[20,128]{1,0:T(8,128)S(1)}, f32[20,128]{1,0:T(8,128)}, u32[]{:S(2)}) copy-start(f32[20,128]{1,0:T(8,128)} %refs_11_.1) | copy-start | bytes 30724
  0.8 88.1 %copy-start.3 = (f32[256,128]{1,0:T(8,128)S(1)}, f32[256,128]{1,0:T(8,128)}, u32[]{:S(2)}) copy-start(f32[256,128]{1,0:T(8,128)} %refs_9_.1) | copy-start | bytes 393220
  0.8 88.1 %copy-start.2 = (f32[256,128]{1,0:T(8,128)S(1)}, f32[256,128]{1,0:T(8,128)}, u32[]{:S(2)}) copy-start(f32[256,128]{1,0:T(8,128)} %refs_8_.1) | copy-start | bytes 393220

commit v2 on v1

--- a/solution.py
+++ b/solution.py
@@ -60,8 +60,11 @@
         self.misc_rows = 64
         self.table_at = 32
 
-    CHUNKS = ((0, 128), (512, 128), (1024, 64), (1280, 128))
-    GRAD_ROWS = 1792
+    BLOCK_ROWS = 320
+    PARTS = ((0, 160), (160, 160))
+    CHUNK = 256
+    PAIRS = (0, 1, 0, 1, 0, 1, None)
+    GRAD_ROWS = 7 * 256
 
     def scratch(self):
         steps, ch = self.steps, self.channels
@@ -69,19 +72,18 @@
         rows = self.GRAD_ROWS
         dma = pltpu.SemaphoreType.DMA
         return dict(
-            ax=pltpu.VMEM((steps + DILATION_SIZE, ch), BF16),
-            mp=pltpu.VMEM((steps, wide), F32),
-            gg=pltpu.VMEM((steps, ch), F32),
+            taps=pltpu.VMEM((2, steps, ch), BF16),
+            halo=pltpu.VMEM((DILATION_SIZE, ch), BF16),
+            act=pltpu.VMEM((steps, wide), F32),
+            own=pltpu.VMEM((2 * self.CHUNK, 4 * LANES), F32),
             gated=pltpu.VMEM((steps, ch), BF16),
             mg=pltpu.VMEM((steps, wide), BF16),
             et=pltpu.VMEM((4 * self.misc_rows, steps), BF16),
+            extra=pltpu.VMEM((steps, 4 * self.misc_rows), BF16),
             cn=pltpu.VMEM((self.cond_dim, steps), BF16),
-            km=pltpu.VMEM((steps, LANES), F32),
-            wb=pltpu.VMEM((4, 2, 128, wide), BF16),
+            km=pltpu.VMEM((steps, LANES), BF16),
+            wall=pltpu.VMEM((4, self.BLOCK_ROWS, wide), BF16),
             wo=pltpu.VMEM((4, 128, wide), BF16),
-            wm=pltpu.VMEM((4, self.misc_rows, wide), BF16),
-            conv_in=pltpu.VMEM((256, LANES), F32),
-            out_in=pltpu.VMEM((128, LANES), F32),
             cond_in=pltpu.VMEM((self.cond_rows, LANES), F32),
             table_in=pltpu.VMEM((self.table_rows, LANES), F32),
             ss=pltpu.VMEM((rows, 4 * LANES), BF16),
@@ -91,19 +93,15 @@
             r3s=pltpu.VMEM((2, rows, LANES), BF16),
             r3r=pltpu.VMEM((2, rows, LANES), BF16),
             zs=pltpu.VMEM((rows, LANES), BF16),
-            zr=pltpu.VMEM((3, rows // 4, LANES), BF16),
+            zr=pltpu.VMEM((3, 4 * 128, LANES), BF16),
             phs=pltpu.VMEM((DILATION_SIZE, ch), BF16),
             phr=pltpu.VMEM((DILATION_SIZE, ch), BF16),
-            nplane=pltpu.VMEM((8, 8, LANES), F32),
-            nline=pltpu.VMEM((4, 8, LANES), F32),
-            g_send=dma((4, 11)),
-            g_recv=dma((4, 11)),
-            r_send=dma((4, 8)),
-            r_recv=dma((4, 8)),
-            n_send=dma((10,)),
-            n_recv=dma((10,)),
-            h_send=dma((2,)),
+            squares=pltpu.VMEM((32, 1, LANES), F32),
+            g_recv=dma((43,)),
+            r_recv=dma((7, 4)),
             h_recv=dma((2,)),
+            sent=dma((7,)),
+            n_recv=dma,
             local=dma((8,)),
         )
 
@@ -115,9 +113,8 @@
         res, skip, agrad, fconv, fmisc, fout, norm = outs
         b = dict(zip(names, bufs))
         steps, ch = self.steps, self.channels
-        ax, mp, gg, gated, mg = b["ax"], b["mp"], b["gg"], b["gated"], b["mg"]
-        et, cn, km, wb, wo, wm = b["et"], b["cn"], b["km"], b["wb"], b["wo"], b["wm"]
-        pv = res
+        taps, act, own, gated, mg = b["taps"], b["act"], b["own"], b["gated"], b["mg"]
+        et, extra, cn, km, wall, wo = b["et"], b["extra"], b["cn"], b["km"], b["wall"], b["wo"]
 
         t = lax.axis_index("tm")
         z = lax.axis_index("batch")
@@ -133,6 +130,7 @@
         zlow, zhigh = lax.rem(z, 2), z // 2
         zdelta = (1 - 2 * zlow, 2 * (1 - 2 * zhigh))
         zpeers = (z + zdelta[0], z + zdelta[1], z + zdelta[0] + zdelta[1])
+        zslab = (z,) + zpeers
         tlow, tmid, thigh = core, xbit, ybit
 
         def lanes(block):
@@ -144,15 +142,19 @@
         def local(i, source, target):
             return pltpu.make_async_copy(source, target, b["local"].at[i])
 
+        def landing(n, size):
+            return act.at[pl.ds(0, size), n * LANES : (n + 1) * LANES]
+
+        conv_in, out_in = landing(0, 256), landing(1, 128)
+        cond_in, table_in = b["cond_in"], b["table_in"]
         small = [
-            local(0, conv_w, b["conv_in"]),
-            local(1, out_w, b["out_in"]),
-            local(2, cond_w, b["cond_in"]),
-            local(3, table_w, b["table_in"]),
+            local(0, conv_w, conv_in),
+            local(1, out_w, out_in),
+            local(2, cond_w, cond_in),
+            local(3, table_w, table_in),
         ]
-        own_ax = ax.at[pl.ds(DILATION_SIZE, steps), :]
         large = [
-            local(4, audio.at[0], own_ax),
+            local(4, audio.at[0], taps.at[1]),
             local(5, conditioning.at[0], cn),
             local(6, grad_res.at[0], agrad),
             local(7, grad_skip.at[0], skip),
@@ -161,104 +163,122 @@
             copy.start()
 
         barrier = pltpu.get_barrier_semaphore()
-        plane = []
-        for k in range(1, 8):
-            dt = (
-                (1 - 2 * tlow) * (k & 1)
-                + 2 * (1 - 2 * tmid) * ((k >> 1) & 1)
-                + 4 * (1 - 2 * thigh) * ((k >> 2) & 1)
-            )
-            plane.append(t + dt)
-        for peer in plane:
-            pl.semaphore_signal(barrier, inc=1, device_id=(peer, z), device_id_type=MESH)
-        for peer in zpeers:
-            pl.semaphore_signal(barrier, inc=1, device_id=(t, peer), device_id_type=MESH)
+        peers = []
+        for k in range(1, 32):
+            pt = t
+            for bit, step in ((tlow, 1), (tmid, 2), (thigh, 4)):
+                if k & step:
+                    pt = pt + step * (1 - 2 * bit)
+            peers.append((pt, zslab[k >> 3]))
+        near = [peer for k, peer in enumerate(peers, 1) if k < 8 or k % 8 == 0]
+        for peer in near:
+            pl.semaphore_signal(barrier, inc=1, device_id=peer, device_id_type=MESH)
         for copy in large:
             copy.start()
 
         for copy in small:
             copy.wait()
-        for h in range(2):
-            wb[z, h, :, lanes(t)] = b["conv_in"][h * 128 : (h + 1) * 128, :].astype(BF16)
-        wo[z, :, lanes(t)] = b["out_in"][...].astype(BF16)
+        wall[z, 0:256, lanes(t)] = conv_in[...].astype(BF16)
+        wo[z, :, lanes(t)] = out_in[...].astype(BF16)
         pad_c = jnp.zeros((self.table_at - self.cond_rows, LANES), F32)
         pad_t = jnp.zeros((self.misc_rows - self.table_at - self.table_rows, LANES), F32)
-        wm[z, :, lanes(t)] = jnp.concatenate(
-            [b["cond_in"][...], pad_c, b["table_in"][...], pad_t], axis=0
+        wall[z, 256 : self.BLOCK_ROWS, lanes(t)] = jnp.concatenate(
+            [cond_in[...], pad_c, table_in[...], pad_t], axis=0
         ).astype(BF16)
-        pl.semaphore_wait(barrier, 10)
-
-        def part(chunk, block, zs=None):
-            whole = zs is None
-            if chunk == 0:
-                return wo.at[:, :, lanes(block)] if whole else wo.at[zs, :, lanes(block)]
-            if chunk == 1:
-                return wm.at[:, :, lanes(block)] if whole else wm.at[zs, :, lanes(block)]
-            h = chunk - 2
-            return wb.at[:, h, :, lanes(block)] if whole else wb.at[zs, h, :, lanes(block)]
-
-        def push(ref, i, chunk, where):
+        pl.semaphore_wait(barrier, len(near))
+
+        def slab(weight, d, block):
+            if weight == 2:
+                return wo.at[pl.ds(zslab[d], 1), :, lanes(block)]
+            row, size = self.PARTS[weight]
+            return wall.at[pl.ds(zslab[d], 1), pl.ds(row, size), lanes(block)]
+
+        def g_copy(unit, block, d, where, arrival):
+            ref = slab(unit, d, block)
             return pltpu.make_async_remote_copy(
                 src_ref=ref,
                 dst_ref=ref,
-                send_sem=b["g_send"].at[chunk, i],
-                recv_sem=b["g_recv"].at[chunk, i],
+                send_sem=b["sent"].at[unit // 2],
+                recv_sem=b["g_recv"].at[arrival],
                 device_id=where,
                 device_id_type=MESH,
             )
 
-        def g_copy(chunk, i):
-            if i < 3:
-                return push(part(chunk, t, pl.ds(z, 1)), i, chunk, (t, zpeers[i]))
-            if i == 3:
-                return push(part(chunk, t), i, chunk, (tx, z))
-            if i == 4:
-                return push(part(chunk, t), i, chunk, (ty, z))
-            if i == 5:
-                return push(part(chunk, tx, pl.ds(0, 2)), i, chunk, (ty, z))
-            if i == 6:
-                return push(part(chunk, ty, pl.ds(2, 2)), i, chunk, (tx, z))
-            block = (t, tx, ty, td)[i - 7] if i < 11 else None
-            return push(part(chunk, block), i, chunk, (sib, z))
-
-        def g_start(chunk, i):
-            g_copy(chunk, i).start()
-
-        def g_wait(chunk, i):
-            g_copy(chunk, i).wait_recv()
-
-        def g_z(chunk):
-            for i in range(3):
-                g_start(chunk, i)
-
-        def g_xy(chunk):
-            for i in range(3):
-                g_wait(chunk, i)
-            for i in (3, 4, 7):
-                g_start(chunk, i)
-
-        def g_f(chunk):
-            g_wait(chunk, 3)
-            g_start(chunk, 5)
-            g_start(chunk, 8)
-            g_wait(chunk, 4)
-            g_start(chunk, 6)
-            g_start(chunk, 9)
-
-        def g_d(chunk):
-            g_wait(chunk, 5)
-            g_wait(chunk, 6)
-            g_start(chunk, 10)
-
-        def g_s(chunk):
-            for i in range(7, 11):
-                g_wait(chunk, i)
+        def g_of(unit, kind, d):
+            if kind == "z":
+                return g_copy(unit, t, 0, (t, zslab[d]), 3 * unit + d - 1 if unit < 2 else 6)
+            if kind in "xyf":
+                n = "xyf".index(kind)
+                block, where = (
+                    ((t, (tx, z)), (t, (ty, z)))[n] if n < 2 else ((tx, (ty, z)), (ty, (tx, z)))[d % 2]
+                )
+                return g_copy(unit, block, d, where, 7 + 8 * n + 4 * unit + d if unit < 2 else 31 + n)
+            column = int(kind[1])
+            arrival = 34 + 2 * column + d // 2 if unit < 2 else 42
+            return g_copy(unit, (t, tx, ty, td)[column], d, (sib, z), arrival)
+
+        def g_start(unit, d, *kinds):
+            for kind in kinds:
+                g_of(unit, kind, d).start()
+
+        def g_z(unit, d):
+            g_of(unit, "z", d).wait_recv()
+            g_start(unit, d, "x", "y", "c0")
+
+        def g_xy(unit, d):
+            g_of(unit, "x", d).wait_recv()
+            g_start(unit, d, *(("f", "c1") if d % 2 == 0 else ("c1",)))
+            g_of(unit, "y", d).wait_recv()
+            g_start(unit, d, *(("f", "c2") if d % 2 == 1 else ("c2",)))
+
+        def g_d(unit, d):
+            g_of(unit, "f", d).wait_recv()
+            g_start(unit, d, "c3")
+
+        def arrived(ref, sem):
+            pltpu.make_async_remote_copy(
+                src_ref=ref,
+                dst_ref=ref,
+                send_sem=b["sent"].at[0],
+                recv_sem=sem,
+                device_id=(sib, z),
+                device_id_type=MESH,
+            ).wait_recv()
+
+        def g_core(column, far):
+            pair = 2 * zhigh if far == 0 else 2 - 2 * zhigh
+            block = (sib, 2 * chip_x + 1 - core, 2 * chip_y + 1 - core, 2 * chip_d + 1 - core)[column]
+            ref = wall.at[pl.ds(pair, 2), :, lanes(block)]
+            arrived(ref, b["g_recv"].at[34 + 2 * column + far])
+
+        def o_first():
+            for d in (1, 2, 3):
+                g_start(2, d, "z")
+
+        def o_xy():
+            arrived(wo.at[0:3, :, lanes(t)], b["g_recv"].at[6])
+            for d in range(4):
+                g_start(2, d, "x", "y", "c0")
+
+        def o_f():
+            arrived(wo.at[:, :, lanes(tx)], b["g_recv"].at[31])
+            arrived(wo.at[:, :, lanes(ty)], b["g_recv"].at[32])
+            for d in range(4):
+                g_start(2, d, "f", "c1", "c2")
+
+        def o_d():
+            arrived(wo.at[:, :, lanes(td)], b["g_recv"].at[33])
+            for d in range(4):
+                g_start(2, d, "c3")
+
+        def o_core():
+            arrived(wo.at[:, :, 0 : 4 * LANES], b["g_recv"].at[42])
 
         def halo_in():
             return pltpu.make_async_remote_copy(
                 src_ref=audio.at[0, pl.ds(steps - DILATION_SIZE, DILATION_SIZE), :],
-                dst_ref=ax.at[pl.ds(0, DILATION_SIZE), :],
-                send_sem=b["h_send"].at[0],
+                dst_ref=b["halo"],
+                send_sem=b["sent"].at[2],
                 recv_sem=b["h_recv"].at[0],
                 device_id=(jnp.minimum(t + 1, 7), z),
                 device_id_type=MESH,
@@ -268,7 +288,7 @@
             return pltpu.make_async_remote_copy(
                 src_ref=b["phs"],
                 dst_ref=b["phr"],
-                send_sem=b["h_send"].at[1],
+                send_sem=b["sent"].at[3],
                 recv_sem=b["h_recv"].at[1],
                 device_id=(jnp.maximum(t - 1, 0), z),
                 device_id_type=MESH,
@@ -278,23 +298,17 @@
             lax.fori_loop(0, count, lambda i, c: (body(i), c)[1], 0)
 
         def make_mask():
-            size = 256
-
-            def body(i):
-                at = rows_at(i * size, size)
-                p = (
-                    t * steps
-                    + i * size
-                    + lax.broadcasted_iota(jnp.int32, (size, LANES), 0)
-                )
+            cut = 1024
+            spread = jnp.where(lax.broadcasted_iota(jnp.int32, (16, LANES), 0) == 0, 1.0, 0.0)
+            for c in range(steps // cut):
+                p = t * steps + c * cut + lax.broadcasted_iota(jnp.int32, (16, cut), 1)
                 drop = None
                 for j in range(self.seg_count):
                     d = p - starts[0, j]
                     hit = (d >= 0) & (d < DILATION_SIZE)
                     drop = hit if drop is None else drop | hit
-                km[at, :] = jnp.where(drop, 0.0, 1.0)
-
-            loop(steps // size, body)
+                keep = jnp.where(drop, 0.0, 1.0).astype(BF16)
+                km[c * cut : (c + 1) * cut, :] = dot_tn(keep, spread.astype(BF16)).astype(BF16)
 
         def make_extra():
             cut = 1024
@@ -315,143 +329,129 @@
                     slot = lax.broadcasted_iota(jnp.int32, (n, cut), 0) - self.table_at
                     ours = (slot >= 0) & (slot < self.table_rows)
                     hot = ours & (slot + q * self.table_rows == wide_speaker)
-                    et[q * n : (q + 1) * n, at] = jnp.where(hot, 1.0, mel).astype(BF16)
+                    part = jnp.where(hot, 1.0, mel)
+                    et[q * n : (q + 1) * n, at] = part.astype(BF16)
+
+        def flip_extra():
+            cut = 1024
+            for c in range(steps // cut):
+                at = pl.ds(c * cut, cut)
+                extra[at, :] = et[:, at].T
 
         def make_prev():
-            size = 512
+            def shift(at, value):
+                keep = jnp.concatenate([km[at, :]] * (ch // LANES), axis=1)
+                taps[0, at, :] = value * keep
+
+            shift(pl.ds(0, DILATION_SIZE), b["halo"][...])
+            size = (steps - DILATION_SIZE) // 4
 
             def body(i):
                 at = rows_at(i * size, size)
-                keep = km[at, :].astype(BF16)
-                pv[at, :] = ax[at, :] * jnp.concatenate([keep] * (ch // LANES), axis=1)
-
-            loop(steps // size, body)
-
-        def gated_grad():
-            size = 1024
+                shift(rows_at(i * size + DILATION_SIZE, size), taps[1, at, :])
+
+            loop(4, body)
+
+        def mixture_first(block):
+            size = steps // 2
+            cols = pl.ds(pl.multiple_of(256 * block, 256), 256)
 
             def body(i):
                 at = rows_at(i * size, size)
-                w = wo[...].reshape(ch, 2 * ch)
-                gg[at, :] = dot_nt(agrad[at, :], w[:, :ch]) + dot_nt(skip[at, :], w[:, ch:])
-
-            loop(steps // size, body)
-
-        def taps(i, size, h):
-            at = rows_at(i * size, size)
-            cur = pl.ds(pl.multiple_of(i * size + DILATION_SIZE, DILATION_SIZE), size)
-            lo = slice(h * 128, h * 128 + 128)
-            hi = slice(256 + h * 128, 256 + h * 128 + 128)
-            return jnp.concatenate([pv[at, lo], pv[at, hi], ax[cur, lo], ax[cur, hi]], axis=1)
-
-        def mixture_first():
-            size = 1024
+                w = wall[pl.ds(2 * zhigh, 2), 0:256, cols].reshape(ch, 256)
+                act[at, cols] = dot_nn(taps[zhigh, at, :], w)
+
+            loop(2, body)
+
+        def mixture(block, other=None):
+            size = steps // 2
+            cols = pl.ds(pl.multiple_of(256 * block, 256), 256)
+            is_gate = block // 2
+            scale = jnp.where(is_gate == 1, 0.5, 1.0).astype(F32)
+            c0 = pl.ds(pl.multiple_of(256 * lax.rem(block, 2), 256), 256)
 
             def body(i):
                 at = rows_at(i * size, size)
-                lhs = taps(i, size, 0)
-                cut = pl.ds(pl.multiple_of(i * size, size), size)
-                for n in range(4):
-                    cols = slice(n * 256, (n + 1) * 256)
-                    w = wb[:, 0, :, cols].reshape(512, 256)
-                    m = wm[:, :, cols].reshape(4 * self.misc_rows, 256)
-                    mp[at, cols] = dot_nn(lhs, w) + dot_tn(et[:, cut], m)
-
-            loop(steps // size, body)
-
-        def gate():
-            size = 1024
-
-            def body(i):
-                at = rows_at(i * size, size)
-                lhs = taps(i, size, 1)
-                for n in range(ch // 256):
-                    c0 = slice(n * 256, (n + 1) * 256)
-                    c1 = slice(ch + n * 256, ch + (n + 1) * 256)
-                    x = mp[at, c0] + dot_nn(lhs, wb[:, 1, :, c0].reshape(512, 256))
-                    y = mp[at, c1] + dot_nn(lhs, wb[:, 1, :, c1].reshape(512, 256))
-                    th = jnp.tanh(x)
-                    sg = 0.5 * jnp.tanh(0.5 * y) + 0.5
-                    q = gg[at, c0]
-                    g = th * sg
-                    gated[at, c0] = g.astype(BF16)
-                    mg[at, c0] = (q * (sg - g * th)).astype(BF16)
-                    mg[at, c1] = (q * (g - g * sg)).astype(BF16)
-
-            loop(steps // size, body)
+                w = wall[pl.ds(2 - 2 * zhigh, 2), 0:256, cols].reshape(ch, 256)
+                m = wall[:, 256 : self.BLOCK_ROWS, cols].reshape(4 * self.misc_rows, 256)
+                x = act[at, cols] + dot_nn(taps[1 - zhigh, at, :], w) + dot_nn(extra[at, :], m)
+                x = scale * jnp.tanh(scale * x) + (1.0 - scale)
+                act[at, cols] = x
+                if other is not None:
+                    y = act[at, pl.ds(pl.multiple_of(256 * other, 256), 256)]
+                    gated[at, c0] = (x * y).astype(BF16)
+
+            loop(2, body)
+
+        def mixture_grad(half):
+            size = 512
+            w = wo[...].reshape(ch, 2 * ch)
+            for i in range(half * 3, half * 3 + 3):
+                at = pl.ds(i * size, size)
+                q = dot_nt(agrad[at, :], w[:, :ch]) + dot_nt(skip[at, :], w[:, ch:])
+                th, sg = act[at, :ch], act[at, ch:]
+                g = th * sg
+                mg[at, :ch] = (q * (sg - g * th)).astype(BF16)
+                mg[at, ch:] = (q * (g - g * sg)).astype(BF16)
 
         def wtaps(first):
-            return wb[first : first + 2].reshape(ch, 2 * ch)
+            return wall[first : first + 2, 0:256, :].reshape(ch, 2 * ch)
 
         def head_back():
             at = pl.ds(0, DILATION_SIZE)
-            keep = jnp.concatenate([km[at, :]] * (ch // LANES), axis=1)
+            keep = jnp.concatenate([km[at, :].astype(F32)] * (ch // LANES), axis=1)
             b["phs"][...] = (keep * dot_nt(mg[at, :], wtaps(0))).astype(BF16)
 
             @pl.when(t > 0)
             def _():
                 halo_back().start()
 
-        def store_grad(row, value):
-            size = value.shape[0]
-            at = pl.ds(row, size)
+        def own_ref(j):
+            return (own, self.CHUNK * j) if j < 2 else (act, self.CHUNK * (j - 2))
+
+        def store_grad(j, value):
+            at = pl.ds(self.CHUNK * j, self.CHUNK)
+            keep, row = own_ref(j)
             even = core == 0
             for k in range(4):
                 left = value[:, 2 * k * LANES : (2 * k + 1) * LANES]
                 right = value[:, (2 * k + 1) * LANES : (2 * k + 2) * LANES]
                 cols = slice(k * LANES, (k + 1) * LANES)
-                mp[at, cols] = jnp.where(even, left, right)
+                keep[pl.ds(row, self.CHUNK), cols] = jnp.where(even, left, right)
                 b["ss"][at, cols] = jnp.where(even, right, left).astype(BF16)
 
-        def conv_grad(h, side):
+        def conv_grad(part):
+            side, h = part % 2, part // 2
             lo = slice(h * 128, h * 128 + 128)
             hi = slice(256 + h * 128, 256 + h * 128 + 128)
-            if side == 0:
-                lhs = jnp.concatenate([pv[:, lo], pv[:, hi]], axis=1)
-            else:
-                cur = pl.ds(DILATION_SIZE, steps)
-                lhs = jnp.concatenate([ax[cur, lo], ax[cur, hi]], axis=1)
-            store_grad(512 * h + 256 * side, dot_tn(lhs, mg[...]))
+            lhs = jnp.concatenate([taps[side, :, lo], taps[side, :, hi]], axis=1)
+            store_grad(2 + part, dot_tn(lhs, mg[...]))
 
         def misc_grad():
-            store_grad(1024, dot_nn(et[...], mg[...]))
-
-        def out_grad(side):
-            lhs = gated[:, side * 256 : (side + 1) * 256]
+            store_grad(6, dot_nn(et[...], mg[...]))
+
+        def out_grad(part):
+            lhs = gated[:, 256 * part : 256 * (part + 1)]
             value = jnp.concatenate([dot_tn(lhs, agrad[...]), dot_tn(lhs, skip[...])], axis=1)
-            store_grad(1280 + 256 * side, value)
-
-        def projected(which):
-            size = 1024
-
-            def body(i):
-                at = rows_at(i * size, size)
-                if which == 0:
-                    w = wo[:, :, :ch].reshape(ch, ch)
-                    cur = pl.ds(pl.multiple_of(i * size + DILATION_SIZE, DILATION_SIZE), size)
-                    res[at, :] = (ax[cur, :].astype(F32) + dot_nn(gated[at, :], w)).astype(BF16)
-                else:
-                    w = wo[:, :, ch:].reshape(ch, ch)
-                    skip[at, :] = dot_nn(gated[at, :], w).astype(BF16)
-
-            loop(steps // size, body)
+            store_grad(part, value)
+
+        def projected(which, i):
+            size = steps // 2
+            cols = slice(which * ch, (which + 1) * ch)
+            at = pl.ds(i * size, size)
+            value = dot_nn(gated[at, :], wo[:, :, cols].reshape(ch, ch))
+            if which == 0:
+                value = value + taps[1, at, :].astype(F32)
+            (res, skip)[which][at, :] = value.astype(BF16)
 
         def audio_block(at, later):
-            keep = jnp.concatenate([km[later, :]] * (ch // LANES), axis=1)
+            keep = jnp.concatenate([km[later, :].astype(F32)] * (ch // LANES), axis=1)
             total = agrad[at, :].astype(F32) + dot_nt(mg[at, :], wtaps(2))
             agrad[at, :] = (total + keep * dot_nt(mg[later, :], wtaps(0))).astype(BF16)
 
-        def audio_main():
-            def body(i):
-                at = rows_at(i * 1024, 1024)
-                later = pl.ds(pl.multiple_of(i * 1024 + DILATION_SIZE, DILATION_SIZE), 1024)
-                audio_block(at, later)
-
-            loop(2, body)
-
-        def audio_rest():
-            size = steps - 2048 - DILATION_SIZE
-            audio_block(pl.ds(2048, size), pl.ds(2048 + DILATION_SIZE, size))
+        def audio_main(i):
+            size = (steps - DILATION_SIZE) // 4
+            audio_block(pl.ds(i * size, size), pl.ds(i * size + DILATION_SIZE, size))
 
         def audio_last():
             @pl.when(t < 7)
@@ -466,139 +466,147 @@
             total = agrad[at, :].astype(F32) + dot_nt(mg[at, :], wtaps(2))
             agrad[at, :] = (total + b["phr"][...].astype(F32)).astype(BF16)
 
-        def r_copy(j, i):
-            row, r = self.CHUNKS[j]
-            if i == 0:
-                at = pl.ds(row, 4 * r)
-                source, target, where = b["ss"].at[at, :], b["sr"].at[at, :], (sib, z)
-            elif i < 3:
-                at = pl.ds(row // 2, 2 * r)
-                source, target = b["r1s"].at[i - 1, at, :], b["r1r"].at[i - 1, at, :]
-                where = (tx, z) if i == 1 else (ty, z)
-            elif i < 5:
-                at = pl.ds(row, 4 * r)
-                source, target = b["r3s"].at[i - 3, at, :], b["r3r"].at[i - 3, at, :]
-                where = (tx, z) if i == 3 else (ty, z)
-            else:
-                peer = zpeers[i - 5]
-                source = b["zs"].at[rows_at(row + peer * r, r), :]
-                target = b["zr"].at[i - 5, pl.ds(row // 4, r), :]
-                where = (t, peer)
+        def r_copy(j, source, target, where, arrival):
             return pltpu.make_async_remote_copy(
                 src_ref=source,
                 dst_ref=target,
-                send_sem=b["r_send"].at[j, i],
-                recv_sem=b["r_recv"].at[j, i],
+                send_sem=b["sent"].at[4 + arrival // 2],
+                recv_sem=b["r_recv"].at[j, arrival],
                 device_id=where,
                 device_id_type=MESH,
             )
 
-        def pair_sum(at, block):
-            return mp[at, lanes(block)] + b["sr"][at, lanes(block)].astype(F32)
+        def r_start(*args):
+            r_copy(*args).start()
+
+        def r_arrived(j, ref, arrival):
+            r_copy(j, ref, ref, (sib, z), arrival).wait_recv()
+
+        def part_rows(j, start, size):
+            return rows_at(self.CHUNK * j + start, size)
+
+        def pair_sum(j, start, size, block):
+            ref, row = own_ref(j)
+            other = b["sr"][part_rows(j, start, size), lanes(block)].astype(F32)
+            return ref[rows_at(row + start, size), lanes(block)] + other
 
         def r_s(j):
-            r_copy(j, 0).start()
+            at = pl.ds(self.CHUNK * j, self.CHUNK)
+            r_start(j, b["ss"].at[at, :], b["sr"].at[at, :], (sib, z), 0)
 
         def r_1(j):
-            row, r = self.CHUNKS[j]
-            r_copy(j, 0).wait_recv()
-            half = pl.ds(row // 2, 2 * r)
-            b["r1s"][0, half, :] = pair_sum(pl.ds(row, 2 * r), chip_d).astype(BF16)
-            r_copy(j, 1).start()
-            b["r1s"][1, half, :] = pair_sum(pl.ds(row + 2 * r, 2 * r), chip_d).astype(BF16)
-            r_copy(j, 2).start()
+            row, half = self.CHUNK * j, self.CHUNK // 2
+            r_arrived(j, b["sr"].at[pl.ds(row, self.CHUNK), :], 0)
+            at = pl.ds(row // 2, half)
+            for i, where in enumerate(((tx, z), (ty, z))):
+                b["r1s"][i, at, :] = pair_sum(j, i * half, half, chip_d).astype(BF16)
+                r_start(j, b["r1s"].at[i, at, :], b["r1r"].at[i, at, :], where, 1)
 
         def r_3(j):
-            row, r = self.CHUNKS[j]
-            up, low = pl.ds(row, 2 * r), pl.ds(row + 2 * r, 2 * r)
-            half = pl.ds(row // 2, 2 * r)
-            b["r3s"][0, up, :] = pair_sum(up, chip_x).astype(BF16)
-            b["r3s"][1, low, :] = pair_sum(low, chip_y).astype(BF16)
-            r_copy(j, 2).wait_recv()
+            row, half = self.CHUNK * j, self.CHUNK // 2
+            up, low = pl.ds(row, half), pl.ds(row + half, half)
+            at, every = pl.ds(row // 2, half), pl.ds(row, self.CHUNK)
+            b["r3s"][0, up, :] = pair_sum(j, 0, half, chip_x).astype(BF16)
+            b["r3s"][1, low, :] = pair_sum(j, half, half, chip_y).astype(BF16)
+            r_arrived(j, b["r1r"].at[:, at, :], 1)
             b["r3s"][0, low, :] = (
-                pair_sum(low, chip_x) + b["r1r"][1, half, :].astype(F32)
+                pair_sum(j, half, half, chip_x) + b["r1r"][1, at, :].astype(F32)
             ).astype(BF16)
-            r_copy(j, 3).start()
-            r_copy(j, 1).wait_recv()
+            r_start(j, b["r3s"].at[0, every, :], b["r3r"].at[0, every, :], (tx, z), 2)
             b["r3s"][1, up, :] = (
-                pair_sum(up, chip_y) + b["r1r"][0, half, :].astype(F32)
+                pair_sum(j, 0, half, chip_y) + b["r1r"][0, at, :].astype(F32)
             ).astype(BF16)
-            r_copy(j, 4).start()
-
-        def plane_sum(at):
+            r_start(j, b["r3s"].at[1, every, :], b["r3r"].at[1, every, :], (ty, z), 2)
+
+        def plane_sum(j, start, size):
+            at = part_rows(j, start, size)
             return (
-                pair_sum(at, chip)
+                pair_sum(j, start, size, chip)
                 + b["r3r"][0, at, :].astype(F32)
                 + b["r3r"][1, at, :].astype(F32)
             )
 
         def final(j):
-            return (fconv.at[pl.ds(0, 128), :], fconv.at[pl.ds(128, 128), :], fmisc, fout)[j]
+            if j < 2:
+                return fout
+            return fconv.at[pl.ds(128 * ((j - 2) // 2), 128), :] if j < 6 else fmisc
+
+        def z_rows(j):
+            return 64 if self.PAIRS[j] is None else 128
+
+        def z_at(j, which):
+            place = which if self.PAIRS[j] is None else lax.rem(which, 2)
+            return place * z_rows(j)
+
+        def z_copy(j, d):
+            at = pl.ds(128 * (j // 2), z_rows(j))
+            return r_copy(
+                j, b["zs"].at[part_rows(j, z_at(j, zslab[d]), z_rows(j)), :], b["zr"].at[d - 1, at, :], (t, zslab[d]), 3
+            )
 
         def r_z(j):
-            row, r = self.CHUNKS[j]
-            r_copy(j, 3).wait_recv()
-            r_copy(j, 4).wait_recv()
-            at = pl.ds(row, 4 * r)
-            b["zs"][at, :] = plane_sum(at).astype(BF16)
-            for i in range(5, 8):
-                r_copy(j, i).start()
-            final(j)[...] = plane_sum(rows_at(row + z * r, r))
+            every = pl.ds(self.CHUNK * j, self.CHUNK)
+            r_arrived(j, b["r3r"].at[:, every, :], 2)
+            b["zs"][every, :] = plane_sum(j, 0, self.CHUNK).astype(BF16)
+            if self.PAIRS[j] is None:
+                for d in (1, 2, 3):
+                    z_copy(j, d).start()
+                final(j)[...] = plane_sum(j, z_at(j, z), z_rows(j))
+                return
+            ours = zhigh == self.PAIRS[j]
+
+            @pl.when(ours)
+            def _():
+                z_copy(j, 1).start()
+                final(j)[...] = plane_sum(j, z_at(j, z), z_rows(j))
+
+            @pl.when(jnp.logical_not(ours))
+            def _():
+                z_copy(j, 2).start()
+                z_copy(j, 3).start()
 
         def r_f(j):
-            row, r = self.CHUNKS[j]
-            total = final(j)[...]
-            for i in range(5, 8):
-                r_copy(j, i).wait_recv()
-                total = total + b["zr"][i - 5, pl.ds(row // 4, r), :].astype(F32)
-            final(j)[...] = total
-
-        def tile_squares():
-            total = jnp.zeros((8, LANES), F32)
-            for j in range(4):
-                value = final(j)[...]
-                total = total + jnp.sum((value * value).reshape(-1, 8, LANES), axis=0)
-            return total
-
-        def n_copy(i):
-            if i < 7:
-                ref, where = b["nplane"].at[t], (plane[i], z)
+            def add():
+                at = pl.ds(128 * (j // 2), z_rows(j))
+                r_arrived(j, b["zr"].at[:, at, :], 3)
+                total = final(j)[...]
+                for i in range(3):
+                    total = total + b["zr"][i, at, :].astype(F32)
+                final(j)[...] = total
+
+            if self.PAIRS[j] is None:
+                add()
             else:
-                ref, where = b["nline"].at[z], (t, zpeers[i - 7])
+                pl.when(zhigh == self.PAIRS[j])(add)
+
+        def n_copy(peer):
+            mine = b["squares"].at[4 * t + z]
             return pltpu.make_async_remote_copy(
-                src_ref=ref,
-                dst_ref=ref,
-                send_sem=b["n_send"].at[i],
-                recv_sem=b["n_recv"].at[i],
-                device_id=where,
+                src_ref=mine,
+                dst_ref=mine,
+                send_sem=b["sent"].at[6],
+                recv_sem=b["n_recv"],
+                device_id=peer,
                 device_id_type=MESH,
             )
 
-        def norm_plane():
-            b["nplane"][t] = tile_squares()
-            for i in range(7):
-                n_copy(i).start()
-
-        def norm_line():
-            for i in range(7):
-                n_copy(i).wait_recv()
-            total = b["nplane"][0]
-            for k in range(1, 8):
-                total = total + b["nplane"][k]
-            b["nline"][z] = total
-            for i in range(7, 10):
-                n_copy(i).start()
+        def norm_start():
+            total = jnp.zeros((8, LANES), F32)
+            for ref in (fconv, fmisc, fout):
+                value = ref[...]
+                total = total + jnp.sum((value * value).reshape(-1, 8, LANES), axis=0)
+            b["squares"][4 * t + z] = jnp.sum(total, axis=0, keepdims=True)
+            for peer in peers:
+                n_copy(peer).start()
 
         def norm_end():
-            for i in range(7, 10):
-                n_copy(i).wait_recv()
-            total = b["nline"][0]
-            for k in range(1, 4):
-                total = total + b["nline"][k]
-            norm[...] = total
-
-        for chunk in (0, 1, 2, 3):
-            g_z(chunk)
+            arrived(b["squares"].at[0:31], b["n_recv"])
+            norm[...] = jnp.sum(b["squares"][...], axis=0)
+
+        for unit in (0, 1):
+            for d in (1, 2, 3):
+                g_start(unit, d, "z")
+            g_start(unit, 0, "x", "y", "c0")
 
         @pl.when(t < 7)
         def _():
@@ -607,84 +615,140 @@
         make_mask()
         large[1].wait()
         make_extra()
+        flip_extra()
+        g_xy(0, 0)
+        g_z(0, 1)
+        g_xy(1, 0)
+        g_z(1, 1)
         large[0].wait()
 
         @pl.when(t == 0)
         def _():
-            ax[pl.ds(0, DILATION_SIZE), :] = jnp.zeros((DILATION_SIZE, ch), BF16)
-
-        g_xy(0)
-        g_xy(1)
-        g_xy(2)
-        g_f(0)
+            b["halo"][...] = jnp.zeros((DILATION_SIZE, ch), BF16)
 
         @pl.when(t > 0)
         def _():
             halo_in().wait_recv()
 
         make_prev()
-        g_xy(3)
-        g_f(1)
-        g_d(0)
-        g_f(2)
+        g_z(0, 2)
+        g_z(1, 2)
+        g_core(0, 0)
+        mixture_first(chip)
+        g_xy(0, 1)
+        g_d(0, 0)
+        g_xy(1, 1)
+        g_d(1, 0)
+        g_z(0, 3)
+        g_z(1, 3)
+        o_first()
+        g_core(2, 0)
+        mixture_first(chip_y)
+        g_xy(0, 2)
+        g_xy(1, 2)
+        g_d(0, 1)
+        g_d(1, 1)
+        g_core(1, 0)
+        mixture_first(chip_x)
+        g_xy(0, 3)
+        g_xy(1, 3)
+        o_xy()
+        g_core(0, 1)
+        mixture(chip)
+        g_d(0, 2)
+        g_d(1, 2)
+        g_core(3, 0)
+        mixture_first(chip_d)
+        g_d(0, 3)
+        g_d(1, 3)
+        g_core(2, 1)
+        mixture(chip_y, chip)
+        g_core(1, 1)
+        mixture(chip_x)
+        o_f()
+        g_core(3, 1)
+        mixture(chip_d, chip_x)
         large[2].wait()
         large[3].wait()
-        g_s(0)
-        gated_grad()
-        g_f(3)
-        g_d(1)
-        g_d(2)
-        g_s(1)
-        g_s(2)
-        mixture_first()
-        g_d(3)
-        g_s(3)
-        gate()
+        out_grad(0)
+        r_s(0)
+        o_d()
+        out_grad(1)
+        r_s(1)
+        r_1(0)
+        o_core()
+        mixture_grad(0)
+        r_1(1)
+        r_3(0)
+        mixture_grad(1)
         head_back()
-        conv_grad(0, 0)
-        conv_grad(0, 1)
-        r_s(0)
-        conv_grad(1, 0)
-        r_1(0)
-        conv_grad(1, 1)
-        r_s(1)
-        r_3(0)
         misc_grad()
+        r_s(6)
+        r_3(1)
+        conv_grad(0)
         r_s(2)
-        r_1(1)
-        out_grad(0)
+        r_1(6)
         r_z(0)
-        r_3(1)
+        conv_grad(1)
+        r_s(3)
+        r_z(1)
         r_1(2)
-        out_grad(1)
-        r_s(3)
+        r_3(6)
+        conv_grad(2)
+        r_s(4)
+        r_1(3)
         r_3(2)
-        audio_main()
-        r_1(3)
-        r_z(1)
+        r_f(0)
+        conv_grad(3)
+        r_s(5)
+        r_z(6)
+        r_1(4)
+        r_3(3)
+        r_f(1)
+        audio_main(0)
+        r_1(5)
         r_z(2)
-        r_f(0)
-        audio_rest()
-        r_3(3)
+        r_3(4)
+        audio_main(1)
+        r_f(6)
+        r_z(3)
+        r_3(5)
+        audio_main(2)
+        r_f(2)
+        audio_main(3)
+        r_z(4)
+        r_f(3)
+        r_z(5)
+        projected(0, 0)
+        projected(0, 1)
+        r_f(4)
+        r_f(5)
+        norm_start()
+        projected(1, 0)
+        projected(1, 1)
         audio_last()
-        r_f(1)
-        projected(0)
-        r_z(3)
-        r_f(2)
-        projected(1)
-        r_f(3)
-        norm_plane()
-        norm_line()
         norm_end()
 
-        for chunk in range(4):
-            for i in range(11):
-                g_copy(chunk, i).wait_send()
-        for j in range(4):
-            for i in range(8):
-                r_copy(j, i).wait_send()
-        for i in range(10):
-            n_copy(i).wait_send()
+        def left(i, ref):
+            pltpu.make_async_remote_copy(
+                src_ref=ref,
+                dst_ref=ref,
+                send_sem=b["sent"].at[i],
+                recv_sem=b["n_recv"],
+                device_id=(sib, z),
+                device_id_type=MESH,
+            ).wait_send()
+
+        row = 2 * ch
+        wall_bytes = 31 * 2 * self.BLOCK_ROWS * LANES
+        wo_bytes = 31 * 2 * 128 * LANES
+        part_bytes = 2 * self.CHUNK * LANES
+        parts = len(self.PAIRS)
+        early = parts * (4 + 1) * part_bytes
+        late = parts * 2 * part_bytes + 9 * part_bytes // 2 + 3 * part_bytes // 4
+        for i, count in ((0, wall_bytes), (1, wo_bytes), (4, early), (5, late)):
+            left(i, taps.at[0, pl.ds(0, count // row), :])
+        left(6, b["squares"].at[0:31])
 
         @pl.when(t < 7)
         def _():
@@ -709,13 +773,13 @@
                 pltpu.VMEM((256, LANES), F32),
                 pltpu.VMEM((self.misc_rows, LANES), F32),
                 pltpu.VMEM((128, LANES), F32),
-                pltpu.VMEM((8, LANES), F32),
+                pltpu.VMEM((1, LANES), F32),
             ],
             in_specs=[smem, smem] + [anywhere] * 8,
             out_specs=[vmem] * 7,
             scratch_shapes=list(self.scratch().values()),
             compiler_params=pltpu.CompilerParams(
-                collective_id=0, has_side_effects=True, vmem_limit_bytes=52 * 2**20
+                collective_id=0, has_side_effects=True, vmem_limit_bytes=54 * 2**20
             ),
             name="layer",
         )(ids, starts, audio, conditioning, grad_res, grad_skip, conv_w, cond_w, table_w, out_w)

time: 93.8 us -> 76.9 us (0.82)
  Pallas kernels: 92.6 us -> 75.7 us
    pallas_call x1, Pallas kernels: 87.9 us -> 71 us  [__call__(): pl.pallas_call(self.kernel, out_shape=[wide, wide, wide, pltpu.VMEM((256,...]
where the time goes in v2:
time: 76.9 us; the launch traced here: 76.7 us
  Pallas kernels  75.7 us (98%)
  between operations  1.03 us (1%)
    pallas_call x1, Pallas kernels, __call__(): pl.pallas_call(self.kernel, out_shape=[wide, wide, wide, pltpu.VMEM((256,...  71 us
    pallas_call x1, Pallas kernels, closing(): pl.pallas_call(functools.partial(closing_kernel, layer.cond_rows, layer.t...  4.65 us

profile of v2, /device:TPU:0, one launch (start us, length us, event | category | flops | bytes accessed | tf_op | source)
XLA Modules:
  0.0 76.7 jit_solution(2689325850876408601)
XLA Ops:
  0.7 0.0 copy-start.1
  0.7 0.0 copy-start.6
  0.7 0.0 copy-start.7
  0.7 0.0 copy-start
  0.7 0.0 copy-start.5
  0.7 0.0 copy-start.4
  0.7 0.0 copy-start.9
  0.7 0.0 copy-start.8
  0.7 0.0 copy-start.11
  0.7 0.0 copy-start.10
  0.8 0.0 copy-start.3
  0.8 0.0 copy-start.2
  0.8 71.0 %layer.1 = (bf16[3072,512]{1,0:T(8,128)(2,1)S(1)}, bf16[3072,512]{1,0:T(8,128)(2,1)S(1)}, bf16[3072,512]{1,0:T(8,128)(2,1)S(1)}, f32[256,128]{1,0:T(8,128)S(1)},...) custom-call(s32[1,8]{1,0:T(1,128)} %ids.1, s32[1,8]{1,0:T(1,128)} %starts.1, ...), custom_call_target="tpu_custom_call" | custom-call | tf_op jit(solution)/shard_map/layer/pallas_call | solution.py:767
  71.8 0.0 copy-done.1
  71.8 0.0 copy-done.6
  71.8 0.0 copy-done.7
  71.8 0.0 copy-done
  71.8 0.0 copy-done.5
  71.8 0.0 copy-done.4
  71.9 0.0 copy-done.9
  71.9 0.0 copy-done.8
  71.9 0.0 copy-done.11
  71.9 0.0 copy-done.10
  71.9 4.6 %closing.1 = (bf16[1,3072,512]{2,1,0:T(8,128)(2,1)}, bf16[1,3072,512]{2,1,0:T(8,128)(2,1)}, bf16[1,3072,512]{2,1,0:T(8,128)(2,1)}, f32[1,1]{1,0:T(1,128)}, f32[2...) custom-call(bf16[3072,512]{1,0:T(8,128)(2,1)S(1)} %get-tuple-element, ...), custom_call_target="tpu_custom_call" | custom-call | tf_op jit(solution)/shard_map/closing/pallas_call | solution.py:820
  (2 shorter events, 0.0 us)
Async XLA Ops:
  0.7 71.1 %copy-start.1 = (f32[128,128]{1,0:T(8,128)S(1)}, f32[128,128]{1,0:T(8,128)}, u32[]{:S(2)}) copy-start(f32[128,128]{1,0:T(8,128)} %refs_16_.1) | copy-start | bytes 196612
  0.7 71.1 %copy-start.6 = (f32[28,128]{1,0:T(8,128)S(1)}, f32[28,128]{1,0:T(8,128)}, u32[]{:S(2)}) copy-start(f32[28,128]{1,0:T(8,128)} %refs_13_.1) | copy-start | bytes 43012
  0.7 71.1 %copy-start.7 = (f32[20,128]{1,0:T(8,128)S(1)}, f32[20,128]{1,0:T(8,128)}, u32[]{:S(2)}) copy-start(f32[20,128]{1,0:T(8,128)} %refs_10_.1) | copy-start | bytes 30724
  0.7 71.1 %copy-start = (f32[256,128]{1,0:T(8,128)S(1)}, f32[256,128]{1,0:T(8,128)}, u32[]{:S(2)}) copy-start(f32[256,128]{1,0:T(8,128)} %refs_7_.1) | copy-start | bytes 393220
  0.7 71.1 %copy-start.5 = (f32[128,128]{1,0:T(8,128)S(1)}, f32[128,128]{1,0:T(8,128)}, u32[]{:S(2)}) copy-start(f32[128,128]{1,0:T(8,128)} %refs_18_.1) | copy-start | bytes 196612
  0.7 71.1 %copy-start.4 = (f32[128,128]{1,0:T(8,128)S(1)}, f32[128,128]{1,0:T(8,128)}, u32[]{:S(2)}) copy-start(f32[128,128]{1,0:T(8,128)} %refs_17_.1) | copy-start | bytes 196612
  0.7 71.1 %copy-start.9 = (f32[28,128]{1,0:T(8,128)S(1)}, f32[28,128]{1,0:T(8,128)}, u32[]{:S(2)}) copy-start(f32[28,128]{1,0:T(8,128)} %refs_15_.1) | copy-start | bytes 43012
  0.7 71.1 %copy-start.8 = (f32[28,128]{1,0:T(8,128)S(1)}, f32[28,128]{1,0:T(8,128)}, u32[]{:S(2)}) copy-start(f32[28,128]{1,0:T(8,128)} %refs_14_.1) | copy-start | bytes 43012
  0.7 71.1 %copy-start.11 = (f32[20,128]{1,0:T(8,128)S(1)}, f32[20,128]{1,0:T(8,128)}, u32[]{:S(2)}) copy-start(f32[20,128]{1,0:T(8,128)} %refs_12_.1) | copy-start | bytes 30724
  0.7 71.1 %copy-start.10 = (f32[20,128]{1,0:T(8,128)S(1)}, f32[20,128]{1,0:T(8,128)}, u32[]{:S(2)}) copy-start(f32[20,128]{1,0:T(8,128)} %refs_11_.1) | copy-start | bytes 30724
  0.8 71.1 %copy-start.3 = (f32[256,128]{1,0:T(8,128)S(1)}, f32[256,128]{1,0:T(8,128)}, u32[]{:S(2)}) copy-start(f32[256,128]{1,0:T(8,128)} %refs_9_.1) | copy-start | bytes 393220
  0.8 71.1 %copy-start.2 = (f32[256,128]{1,0:T(8,128)S(1)}, f32[256,128]{1,0:T(8,128)}, u32[]{:S(2)}) copy-start(f32[256,128]{1,0:T(8,128)} %refs_8_.1) | copy-start | bytes 393220

commit v3 on v2

--- a/solution.py
+++ b/solution.py
@@ -61,9 +61,7 @@
         self.table_at = 32
 
     BLOCK_ROWS = 320
-    PARTS = ((0, 160), (160, 160))
-    CHUNK = 256
-    PAIRS = (0, 1, 0, 1, 0, 1, None)
+    PARTS = tuple((256 * j, 256, j % 2) for j in range(6)) + ((1536, 128, 0), (1664, 128, 1))
     GRAD_ROWS = 7 * 256
 
     def scratch(self):
@@ -75,7 +73,7 @@
             taps=pltpu.VMEM((2, steps, ch), BF16),
             halo=pltpu.VMEM((DILATION_SIZE, ch), BF16),
             act=pltpu.VMEM((steps, wide), F32),
-            own=pltpu.VMEM((2 * self.CHUNK, 4 * LANES), F32),
+            own=pltpu.VMEM((512, 4 * LANES), F32),
             gated=pltpu.VMEM((steps, ch), BF16),
             mg=pltpu.VMEM((steps, wide), BF16),
             et=pltpu.VMEM((4 * self.misc_rows, steps), BF16),
@@ -84,6 +82,8 @@
             km=pltpu.VMEM((steps, LANES), BF16),
             wall=pltpu.VMEM((4, self.BLOCK_ROWS, wide), BF16),
             wo=pltpu.VMEM((4, 128, wide), BF16),
+            ids=pltpu.SMEM((1, self.seg_count), jnp.int32),
+            starts=pltpu.SMEM((1, self.seg_count), jnp.int32),
             cond_in=pltpu.VMEM((self.cond_rows, LANES), F32),
             table_in=pltpu.VMEM((self.table_rows, LANES), F32),
             ss=pltpu.VMEM((rows, 4 * LANES), BF16),
@@ -97,16 +97,16 @@
             phs=pltpu.VMEM((DILATION_SIZE, ch), BF16),
             phr=pltpu.VMEM((DILATION_SIZE, ch), BF16),
             squares=pltpu.VMEM((32, 1, LANES), F32),
-            g_recv=dma((43,)),
-            r_recv=dma((7, 4)),
+            g_recv=dma((33,)),
+            r_recv=dma((8, 4)),
             h_recv=dma((2,)),
             sent=dma((7,)),
             n_recv=dma,
-            local=dma((8,)),
+            local=dma((10,)),
         )
 
     def kernel(
-        self, ids, starts, audio, conditioning, grad_res, grad_skip, conv_w, cond_w, table_w, out_w, *rest
+        self, ids_in, starts_in, audio, conditioning, grad_res, grad_skip, conv_w, cond_w, table_w, out_w, *rest
     ):
         names = list(self.scratch())
         outs, bufs = rest[: len(rest) - len(names)], rest[len(rest) - len(names) :]
@@ -114,6 +114,7 @@
         b = dict(zip(names, bufs))
         steps, ch = self.steps, self.channels
         taps, act, own, gated, mg = b["taps"], b["act"], b["own"], b["gated"], b["mg"]
+        ids, starts = b["ids"], b["starts"]
         et, extra, cn, km, wall, wo = b["et"], b["extra"], b["cn"], b["km"], b["wall"], b["wo"]
 
         t = lax.axis_index("tm")
@@ -159,7 +160,8 @@
             local(6, grad_res.at[0], agrad),
             local(7, grad_skip.at[0], skip),
         ]
-        for copy in small:
+        scalars = [local(8, starts_in, starts), local(9, ids_in, ids)]
+        for copy in small + scalars:
             copy.start()
 
         barrier = pltpu.get_barrier_semaphore()
@@ -176,6 +178,9 @@
         for copy in large:
             copy.start()
 
+        def barrier_wait():
+            pl.semaphore_wait(barrier, len(near))
+
         for copy in small:
             copy.wait()
         wall[z, 0:256, lanes(t)] = conv_in[...].astype(BF16)
@@ -185,55 +190,63 @@
         wall[z, 256 : self.BLOCK_ROWS, lanes(t)] = jnp.concatenate(
             [cond_in[...], pad_c, table_in[...], pad_t], axis=0
         ).astype(BF16)
-        pl.semaphore_wait(barrier, len(near))
-
-        def slab(weight, d, block):
-            if weight == 2:
+        def slab(unit, e, block):
+            d = min(e, 3)
+            if unit == 1:
                 return wo.at[pl.ds(zslab[d], 1), :, lanes(block)]
-            row, size = self.PARTS[weight]
-            return wall.at[pl.ds(zslab[d], 1), pl.ds(row, size), lanes(block)]
-
-        def g_copy(unit, block, d, where, arrival):
-            ref = slab(unit, d, block)
+            size = self.BLOCK_ROWS if e < 3 else self.BLOCK_ROWS // 2
+            return wall.at[pl.ds(zslab[d], 1), pl.ds(size if e == 4 else 0, size), lanes(block)]
+
+        def g_copy(unit, ref, where, arrival):
             return pltpu.make_async_remote_copy(
                 src_ref=ref,
                 dst_ref=ref,
-                send_sem=b["sent"].at[unit // 2],
+                send_sem=b["sent"].at[unit],
                 recv_sem=b["g_recv"].at[arrival],
                 device_id=where,
                 device_id_type=MESH,
             )
 
-        def g_of(unit, kind, d):
+        def g_of(unit, kind, e):
             if kind == "z":
-                return g_copy(unit, t, 0, (t, zslab[d]), 3 * unit + d - 1 if unit < 2 else 6)
+                ref = slab(unit, 0, t)
+                if unit == 0 and e >= 3:
+                    size = self.BLOCK_ROWS // 2
+                    ref = wall.at[pl.ds(z, 1), pl.ds((e - 3) * size, size), lanes(t)]
+                return g_copy(unit, ref, (t, zslab[min(e, 3)]), 4 if unit else e - 1)
+            if kind == "k":
+                return g_copy(unit, slab(unit, 0, td), (t, zslab[1]), 16)
             if kind in "xyf":
                 n = "xyf".index(kind)
-                block, where = (
-                    ((t, (tx, z)), (t, (ty, z)))[n] if n < 2 else ((tx, (ty, z)), (ty, (tx, z)))[d % 2]
-                )
-                return g_copy(unit, block, d, where, 7 + 8 * n + 4 * unit + d if unit < 2 else 31 + n)
+                if kind == "f":
+                    block, where = ((tx, (ty, z)), (ty, (tx, z)))[min(e, 3) % 2]
+                else:
+                    block, where = t, ((tx, z), (ty, z))[n]
+                return g_copy(unit, slab(unit, e, block), where, 20 + n if unit else 5 + 5 * n + e)
             column = int(kind[1])
-            arrival = 34 + 2 * column + d // 2 if unit < 2 else 42
-            return g_copy(unit, (t, tx, ty, td)[column], d, (sib, z), arrival)
-
-        def g_start(unit, d, *kinds):
+            arrival = 31 if unit else 23 + 2 * column + min(e, 3) // 2
+            return g_copy(unit, slab(unit, e, (t, tx, ty, td)[column]), (sib, z), arrival)
+
+        def g_start(unit, e, *kinds):
             for kind in kinds:
-                g_of(unit, kind, d).start()
-
-        def g_z(unit, d):
-            g_of(unit, "z", d).wait_recv()
-            g_start(unit, d, "x", "y", "c0")
-
-        def g_xy(unit, d):
-            g_of(unit, "x", d).wait_recv()
-            g_start(unit, d, *(("f", "c1") if d % 2 == 0 else ("c1",)))
-            g_of(unit, "y", d).wait_recv()
-            g_start(unit, d, *(("f", "c2") if d % 2 == 1 else ("c2",)))
-
-        def g_d(unit, d):
-            g_of(unit, "f", d).wait_recv()
-            g_start(unit, d, "c3")
+                g_of(unit, kind, e).start()
+
+        def g_z(e):
+            g_of(0, "z", e).wait_recv()
+            g_start(0, e, "x", "y", "c0")
+
+        def g_xy(e):
+            g_of(0, "x", e).wait_recv()
+            g_start(0, e, *(("f", "c1") if e in (0, 2) else ("c1",)))
+            g_of(0, "y", e).wait_recv()
+            g_start(0, e, *(("f", "c2") if e >= 3 else ("c2",)))
+
+        def g_d(e):
+            if e == 1:
+                g_copy(0, slab(0, 1, td), (t, zslab[1]), 16).wait_recv()
+            else:
+                g_of(0, "f", e).wait_recv()
+            g_start(0, e, *(("k", "c3") if e == 0 else ("c3",)))
 
         def arrived(ref, sem):
             pltpu.make_async_remote_copy(
@@ -249,30 +262,31 @@
             pair = 2 * zhigh if far == 0 else 2 - 2 * zhigh
             block = (sib, 2 * chip_x + 1 - core, 2 * chip_y + 1 - core, 2 * chip_d + 1 - core)[column]
             ref = wall.at[pl.ds(pair, 2), :, lanes(block)]
-            arrived(ref, b["g_recv"].at[34 + 2 * column + far])
+            arrived(ref, b["g_recv"].at[23 + 2 * column + far])
 
         def o_first():
+            g_start(1, 0, "x", "y", "c0")
+
+        def o_xy():
+            g_of(1, "x", 0).wait_recv()
+            g_start(1, 0, "f", "c1")
+            g_of(1, "y", 0).wait_recv()
+            g_start(1, 0, "c2")
+
+        def o_z():
+            g_of(1, "f", 0).wait_recv()
+            g_start(1, 0, "c3")
+            for d in (2, 3, 1):
+                for block in (t, tx, ty, td):
+                    g_copy(1, slab(1, 0, block), (t, zslab[d]), 4).start()
+
+        def o_d():
+            arrived(wo.at[0:3, :, 0 : 4 * LANES], b["g_recv"].at[4])
             for d in (1, 2, 3):
-                g_start(2, d, "z")
-
-        def o_xy():
-            arrived(wo.at[0:3, :, lanes(t)], b["g_recv"].at[6])
-            for d in range(4):
-                g_start(2, d, "x", "y", "c0")
-
-        def o_f():
-            arrived(wo.at[:, :, lanes(tx)], b["g_recv"].at[31])
-            arrived(wo.at[:, :, lanes(ty)], b["g_recv"].at[32])
-            for d in range(4):
-                g_start(2, d, "f", "c1", "c2")
-
-        def o_d():
-            arrived(wo.at[:, :, lanes(td)], b["g_recv"].at[33])
-            for d in range(4):
-                g_start(2, d, "c3")
+                g_start(1, d, "c0", "c1", "c2", "c3")
 
         def o_core():
-            arrived(wo.at[:, :, 0 : 4 * LANES], b["g_recv"].at[42])
+            arrived(wo.at[:, :, 0 : 4 * LANES], b["g_recv"].at[31])
 
         def halo_in():
             return pltpu.make_async_remote_copy(
@@ -338,12 +352,14 @@
                 at = pl.ds(c * cut, cut)
                 extra[at, :] = et[:, at].T
 
-        def make_prev():
-            def shift(at, value):
-                keep = jnp.concatenate([km[at, :]] * (ch // LANES), axis=1)
-                taps[0, at, :] = value * keep
-
+        def shift(at, value):
+            keep = jnp.concatenate([km[at, :]] * (ch // LANES), axis=1)
+            taps[0, at, :] = value * keep
+
+        def prev_head():
             shift(pl.ds(0, DILATION_SIZE), b["halo"][...])
+
+        def prev_rest():
             size = (steps - DILATION_SIZE) // 4
 
             def body(i):
@@ -352,26 +368,29 @@
 
             loop(4, body)
 
-        def mixture_first(block):
-            size = steps // 2
+        body_rows = steps - DILATION_SIZE
+
+        def mixture_first(block, between=lambda: None):
+            size = body_rows // 2
             cols = pl.ds(pl.multiple_of(256 * block, 256), 256)
 
             def body(i):
-                at = rows_at(i * size, size)
+                at = rows_at(i * size + DILATION_SIZE, size)
                 w = wall[pl.ds(2 * zhigh, 2), 0:256, cols].reshape(ch, 256)
                 act[at, cols] = dot_nn(taps[zhigh, at, :], w)
+                pl.when(i == 0)(between)
 
             loop(2, body)
 
-        def mixture(block, other=None):
-            size = steps // 2
+        def mixture(block, other=None, between=lambda: None):
+            size = body_rows // 2
             cols = pl.ds(pl.multiple_of(256 * block, 256), 256)
             is_gate = block // 2
             scale = jnp.where(is_gate == 1, 0.5, 1.0).astype(F32)
             c0 = pl.ds(pl.multiple_of(256 * lax.rem(block, 2), 256), 256)
 
             def body(i):
-                at = rows_at(i * size, size)
+                at = rows_at(i * size + DILATION_SIZE, size)
                 w = wall[pl.ds(2 - 2 * zhigh, 2), 0:256, cols].reshape(ch, 256)
                 m = wall[:, 256 : self.BLOCK_ROWS, cols].reshape(4 * self.misc_rows, 256)
                 x = act[at, cols] + dot_nn(taps[1 - zhigh, at, :], w) + dot_nn(extra[at, :], m)
@@ -380,6 +399,27 @@
                 if other is not None:
                     y = act[at, pl.ds(pl.multiple_of(256 * other, 256), 256)]
                     gated[at, c0] = (x * y).astype(BF16)
+                pl.when(i == 0)(between)
+
+            loop(2, body)
+
+        def mixture_head():
+            at = pl.ds(0, DILATION_SIZE)
+
+            def body(i):
+                def columns(block):
+                    cols = pl.ds(pl.multiple_of(256 * block, 256), 256)
+                    w = wall[:, 0:256, cols].reshape(2 * ch, 256)
+                    m = wall[:, 256 : self.BLOCK_ROWS, cols].reshape(4 * self.misc_rows, 256)
+                    x = dot_nn(taps[0, at, :], w[:ch]) + dot_nn(taps[1, at, :], w[ch:])
+                    return cols, x + dot_nn(extra[at, :], m)
+
+                c0, x = columns(i)
+                c1, y = columns(i + 2)
+                th, sg = jnp.tanh(x), 0.5 * jnp.tanh(0.5 * y) + 0.5
+                act[at, c0] = th
+                act[at, c1] = sg
+                gated[at, c0] = (th * sg).astype(BF16)
 
             loop(2, body)
 
@@ -402,22 +442,23 @@
             keep = jnp.concatenate([km[at, :].astype(F32)] * (ch // LANES), axis=1)
             b["phs"][...] = (keep * dot_nt(mg[at, :], wtaps(0))).astype(BF16)
 
+        def head_send():
             @pl.when(t > 0)
             def _():
                 halo_back().start()
 
-        def own_ref(j):
-            return (own, self.CHUNK * j) if j < 2 else (act, self.CHUNK * (j - 2))
-
-        def store_grad(j, value):
-            at = pl.ds(self.CHUNK * j, self.CHUNK)
-            keep, row = own_ref(j)
+        def own_ref(row):
+            return (own, row) if row < 512 else (act, row - 512)
+
+        def store_grad(start, value):
+            at = pl.ds(start, 256)
+            keep, row = own_ref(start)
             even = core == 0
             for k in range(4):
                 left = value[:, 2 * k * LANES : (2 * k + 1) * LANES]
                 right = value[:, (2 * k + 1) * LANES : (2 * k + 2) * LANES]
                 cols = slice(k * LANES, (k + 1) * LANES)
-                keep[pl.ds(row, self.CHUNK), cols] = jnp.where(even, left, right)
+                keep[pl.ds(row, 256), cols] = jnp.where(even, left, right)
                 b["ss"][at, cols] = jnp.where(even, right, left).astype(BF16)
 
         def conv_grad(part):
@@ -425,15 +466,15 @@
             lo = slice(h * 128, h * 128 + 128)
             hi = slice(256 + h * 128, 256 + h * 128 + 128)
             lhs = jnp.concatenate([taps[side, :, lo], taps[side, :, hi]], axis=1)
-            store_grad(2 + part, dot_tn(lhs, mg[...]))
+            store_grad(512 + 256 * part, dot_tn(lhs, mg[...]))
 
         def misc_grad():
-            store_grad(6, dot_nn(et[...], mg[...]))
+            store_grad(1536, dot_nn(et[...], mg[...]))
 
         def out_grad(part):
             lhs = gated[:, 256 * part : 256 * (part + 1)]
             value = jnp.concatenate([dot_tn(lhs, agrad[...]), dot_tn(lhs, skip[...])], axis=1)
-            store_grad(part, value)
+            store_grad(256 * part, value)
 
         def projected(which, i):
             size = steps // 2
@@ -483,29 +524,31 @@
             r_copy(j, ref, ref, (sib, z), arrival).wait_recv()
 
         def part_rows(j, start, size):
-            return rows_at(self.CHUNK * j + start, size)
+            return rows_at(self.PARTS[j][0] + start, size)
 
         def pair_sum(j, start, size, block):
-            ref, row = own_ref(j)
+            ref, row = own_ref(self.PARTS[j][0])
             other = b["sr"][part_rows(j, start, size), lanes(block)].astype(F32)
             return ref[rows_at(row + start, size), lanes(block)] + other
 
         def r_s(j):
-            at = pl.ds(self.CHUNK * j, self.CHUNK)
+            at = part_rows(j, 0, self.PARTS[j][1])
             r_start(j, b["ss"].at[at, :], b["sr"].at[at, :], (sib, z), 0)
 
         def r_1(j):
-            row, half = self.CHUNK * j, self.CHUNK // 2
-            r_arrived(j, b["sr"].at[pl.ds(row, self.CHUNK), :], 0)
+            row, size, _ = self.PARTS[j]
+            half = size // 2
+            r_arrived(j, b["sr"].at[pl.ds(row, size), :], 0)
             at = pl.ds(row // 2, half)
             for i, where in enumerate(((tx, z), (ty, z))):
                 b["r1s"][i, at, :] = pair_sum(j, i * half, half, chip_d).astype(BF16)
                 r_start(j, b["r1s"].at[i, at, :], b["r1r"].at[i, at, :], where, 1)
 
         def r_3(j):
-            row, half = self.CHUNK * j, self.CHUNK // 2
+            row, size, _ = self.PARTS[j]
+            half = size // 2
             up, low = pl.ds(row, half), pl.ds(row + half, half)
-            at, every = pl.ds(row // 2, half), pl.ds(row, self.CHUNK)
+            at, every = pl.ds(row // 2, half), pl.ds(row, size)
             b["r3s"][0, up, :] = pair_sum(j, 0, half, chip_x).astype(BF16)
             b["r3s"][1, low, :] = pair_sum(j, half, half, chip_y).astype(BF16)
             r_arrived(j, b["r1r"].at[:, at, :], 1)
@@ -531,53 +574,41 @@
                 return fout
             return fconv.at[pl.ds(128 * ((j - 2) // 2), 128), :] if j < 6 else fmisc
 
-        def z_rows(j):
-            return 64 if self.PAIRS[j] is None else 128
-
         def z_at(j, which):
-            place = which if self.PAIRS[j] is None else lax.rem(which, 2)
-            return place * z_rows(j)
+            half = self.PARTS[j][1] // 2
+            return lax.rem(which, 2) * half, half
+
+        def z_slot(j):
+            return pl.ds(128 * (j // 2), self.PARTS[j][1] // 2)
 
         def z_copy(j, d):
-            at = pl.ds(128 * (j // 2), z_rows(j))
-            return r_copy(
-                j, b["zs"].at[part_rows(j, z_at(j, zslab[d]), z_rows(j)), :], b["zr"].at[d - 1, at, :], (t, zslab[d]), 3
-            )
+            source = b["zs"].at[part_rows(j, *z_at(j, zslab[d])), :]
+            return r_copy(j, source, b["zr"].at[d - 1, z_slot(j), :], (t, zslab[d]), 3)
 
         def r_z(j):
-            every = pl.ds(self.CHUNK * j, self.CHUNK)
+            row, size, pair = self.PARTS[j]
+            every = pl.ds(row, size)
             r_arrived(j, b["r3r"].at[:, every, :], 2)
-            b["zs"][every, :] = plane_sum(j, 0, self.CHUNK).astype(BF16)
-            if self.PAIRS[j] is None:
-                for d in (1, 2, 3):
-                    z_copy(j, d).start()
-                final(j)[...] = plane_sum(j, z_at(j, z), z_rows(j))
-                return
-            ours = zhigh == self.PAIRS[j]
-
-            @pl.when(ours)
+            b["zs"][every, :] = plane_sum(j, 0, size).astype(BF16)
+
+            @pl.when(zhigh == pair)
             def _():
                 z_copy(j, 1).start()
-                final(j)[...] = plane_sum(j, z_at(j, z), z_rows(j))
-
-            @pl.when(jnp.logical_not(ours))
+                final(j)[...] = plane_sum(j, *z_at(j, z))
+
+            @pl.when(zhigh != pair)
             def _():
                 z_copy(j, 2).start()
                 z_copy(j, 3).start()
 
         def r_f(j):
-            def add():
-                at = pl.ds(128 * (j // 2), z_rows(j))
-                r_arrived(j, b["zr"].at[:, at, :], 3)
+            @pl.when(zhigh == self.PARTS[j][2])
+            def _():
+                r_arrived(j, b["zr"].at[:, z_slot(j), :], 3)
                 total = final(j)[...]
                 for i in range(3):
-                    total = total + b["zr"][i, at, :].astype(F32)
+                    total = total + b["zr"][i, z_slot(j), :].astype(F32)
                 final(j)[...] = total
-
-            if self.PAIRS[j] is None:
-                add()
-            else:
-                pl.when(zhigh == self.PAIRS[j])(add)
 
         def n_copy(peer):
             mine = b["squares"].at[4 * t + z]
@@ -596,31 +627,64 @@
                 value = ref[...]
                 total = total + jnp.sum((value * value).reshape(-1, 8, LANES), axis=0)
             b["squares"][4 * t + z] = jnp.sum(total, axis=0, keepdims=True)
-            for peer in peers:
+            for peer in reversed(peers):
                 n_copy(peer).start()
 
         def norm_end():
             arrived(b["squares"].at[0:31], b["n_recv"])
             norm[...] = jnp.sum(b["squares"][...], axis=0)
 
-        for unit in (0, 1):
-            for d in (1, 2, 3):
-                g_start(unit, d, "z")
-            g_start(unit, 0, "x", "y", "c0")
+        for copy in scalars:
+            copy.wait()
+        make_mask()
+        barrier_wait()
+        g_start(0, 0, "x", "y")
+        g_start(0, 1, "z")
+        g_start(0, 0, "c0")
+        g_start(0, 2, "z")
+        large[1].wait()
+        make_extra()
+        g_start(0, 3, "z")
+        g_start(0, 4, "z")
+        flip_extra()
+        o_first()
+        large[0].wait()
+        prev_rest()
+        g_xy(0)
+        g_z(1)
+        g_core(0, 0)
+        mixture_first(chip, lambda: g_z(2))
+        o_xy()
+        g_d(0)
+        g_z(3)
+        g_xy(1)
+        g_z(4)
+        g_core(2, 0)
+        mixture_first(chip_y)
+        g_xy(2)
+        o_z()
+        g_core(1, 0)
+        mixture_first(chip_x)
+        g_xy(3)
+        g_xy(4)
 
         @pl.when(t < 7)
         def _():
             halo_in().start()
 
-        make_mask()
-        large[1].wait()
-        make_extra()
-        flip_extra()
-        g_xy(0, 0)
-        g_z(0, 1)
-        g_xy(1, 0)
-        g_z(1, 1)
-        large[0].wait()
+        g_d(1)
+        g_core(0, 1)
+        mixture(chip)
+        g_d(2)
+        g_core(3, 0)
+        mixture_first(chip_d)
+        g_core(2, 1)
+        mixture(chip_y, chip, lambda: g_d(3))
+        g_d(4)
+        g_core(1, 1)
+        mixture(chip_x)
+        g_core(3, 1)
+        mixture(chip_d, chip_x)
 
         @pl.when(t == 0)
         def _():
@@ -630,101 +694,71 @@
         def _():
             halo_in().wait_recv()
 
-        make_prev()
-        g_z(0, 2)
-        g_z(1, 2)
-        g_core(0, 0)
-        mixture_first(chip)
-        g_xy(0, 1)
-        g_d(0, 0)
-        g_xy(1, 1)
-        g_d(1, 0)
-        g_z(0, 3)
-        g_z(1, 3)
-        o_first()
-        g_core(2, 0)
-        mixture_first(chip_y)
-        g_xy(0, 2)
-        g_xy(1, 2)
-        g_d(0, 1)
-        g_d(1, 1)
-        g_core(1, 0)
-        mixture_first(chip_x)
-        g_xy(0, 3)
-        g_xy(1, 3)
-        o_xy()
-        g_core(0, 1)
-        mixture(chip)
-        g_d(0, 2)
-        g_d(1, 2)
-        g_core(3, 0)
-        mixture_first(chip_d)
-        g_d(0, 3)
-        g_d(1, 3)
-        g_core(2, 1)
-        mixture(chip_y, chip)
-        g_core(1, 1)
-        mixture(chip_x)
-        o_f()
-        g_core(3, 1)
-        mixture(chip_d, chip_x)
+        prev_head()
+        mixture_head()
         large[2].wait()
         large[3].wait()
         out_grad(0)
         r_s(0)
         o_d()
         out_grad(1)
+        r_1(0)
         r_s(1)
-        r_1(0)
         o_core()
         mixture_grad(0)
         r_1(1)
+        mixture_grad(1)
         r_3(0)
-        mixture_grad(1)
+        conv_grad(0)
+        r_3(1)
+        r_s(2)
+        conv_grad(1)
+        r_1(2)
+        r_s(3)
+        conv_grad(2)
+        r_z(0)
+        r_1(3)
+        r_s(4)
+        conv_grad(3)
+        r_3(2)
+        r_z(1)
+        r_1(4)
+        r_s(5)
+        misc_grad()
+        r_3(3)
+        r_1(5)
+        r_s(6)
+        r_s(7)
         head_back()
-        misc_grad()
-        r_s(6)
-        r_3(1)
-        conv_grad(0)
-        r_s(2)
+        r_3(4)
+        r_f(0)
+        projected(0, 0)
         r_1(6)
-        r_z(0)
-        conv_grad(1)
-        r_s(3)
-        r_z(1)
-        r_1(2)
+        r_1(7)
+        r_z(2)
+        audio_main(0)
+        r_3(5)
+        r_z(3)
+        r_f(1)
+        projected(0, 1)
         r_3(6)
-        conv_grad(2)
-        r_s(4)
-        r_1(3)
-        r_3(2)
-        r_f(0)
-        conv_grad(3)
-        r_s(5)
+        r_3(7)
+        head_send()
+        r_z(4)
+        audio_main(1)
+        r_z(5)
+        r_f(2)
+        projected(1, 0)
+        r_f(3)
         r_z(6)
-        r_1(4)
-        r_3(3)
-        r_f(1)
-        audio_main(0)
-        r_1(5)
-        r_z(2)
-        r_3(4)
-        audio_main(1)
+        r_z(7)
+        audio_main(2)
+        r_f(4)
+        audio_main(3)
+        r_f(5)
         r_f(6)
-        r_z(3)
-        r_3(5)
-        audio_main(2)
-        r_f(2)
-        audio_main(3)
-        r_z(4)
-        r_f(3)
-        r_z(5)
-        projected(0, 0)
-        projected(0, 1)
-        r_f(4)
-        r_f(5)
+        r_f(7)
         norm_start()
-        projected(1, 0)
         projected(1, 1)
         audio_last()
         norm_end()
@@ -742,10 +776,9 @@
         row = 2 * ch
         wall_bytes = 31 * 2 * self.BLOCK_ROWS * LANES
         wo_bytes = 31 * 2 * 128 * LANES
-        part_bytes = 2 * self.CHUNK * LANES
-        parts = len(self.PAIRS)
-        early = parts * (4 + 1) * part_bytes
-        late = parts * 2 * part_bytes + 9 * part_bytes // 2 + 3 * part_bytes // 4
+        block_bytes = 2 * self.GRAD_ROWS * LANES
+        early = 5 * block_bytes
+        late = 2 * block_bytes + 3 * block_bytes // 4
         for i, count in ((0, wall_bytes), (1, wo_bytes), (4, early), (5, late)):
             left(i, taps.at[0, pl.ds(0, count // row), :])
         left(6, b["squares"].at[0:31])
@@ -761,7 +794,6 @@
     def __call__(self, ids, starts, audio, conditioning, grad_res, grad_skip, conv_w, cond_w, table_w, out_w):
         steps, ch = self.steps, self.channels
         wide = pltpu.VMEM((steps, ch), BF16)
-        smem = pl.BlockSpec(memory_space=pltpu.SMEM)
         anywhere = pl.BlockSpec(memory_space=pl.ANY)
         vmem = pl.BlockSpec(memory_space=pltpu.VMEM)
         return pl.pallas_call(
@@ -775,7 +807,7 @@
                 pltpu.VMEM((128, LANES), F32),
                 pltpu.VMEM((1, LANES), F32),
             ],
-            in_specs=[smem, smem] + [anywhere] * 8,
+            in_specs=[anywhere] * 10,
             out_specs=[vmem] * 7,
             scratch_shapes=list(self.scratch().values()),
             compiler_params=pltpu.CompilerParams(
@@ -789,13 +821,15 @@
     (res, skip, agrad, fconv, fmisc, fout, norm), refs = refs[:7], refs[7:]
     state, refs = refs[:12], refs[12:]
     (res_o, skip_o, agrad_o, prenorm_o), refs = refs[:4], refs[4:]
-    new, (sems,) = refs[:12], refs[12:]
-    copies = [
-        pltpu.make_async_copy(source, target.at[0], sems.at[i])
-        for i, (source, target) in enumerate(((res, res_o), (skip, skip_o), (agrad, agrad_o)))
-    ]
-    for copy in copies:
-        copy.start()
+    new_o, new, (sems,) = refs[:12], refs[12:24], refs[24:]
+    copies = []
+
+    def write(source, target):
+        copies.append(pltpu.make_async_copy(source, target, sems.at[len(copies)]))
+        copies[-1].start()
+
+    for source, target in ((res, res_o), (skip, skip_o), (agrad, agrad_o)):
+        write(source, target.at[0])
     prenorm = jnp.sqrt(jnp.sum(norm[...], keepdims=True))
     prenorm_o[...] = prenorm
     factor = jnp.minimum(1.0, clip_level / (prenorm + 1e-06))
@@ -809,6 +843,7 @@
         master, first, second = (state[3 * k + i][...] for i in range(3))
         for i, value in enumerate(adamw(grad, factor, master, first, second)):
             new[3 * k + i][...] = value
+            write(new[3 * k + i], new_o[3 * k + i])
     for copy in copies:
         copy.wait()
 
@@ -822,8 +857,8 @@
         out_shape=[wide, wide, wide, jax.ShapeDtypeStruct((1, 1), F32)]
         + [jax.ShapeDtypeStruct(a.shape, F32) for a in state],
         in_specs=[vmem] * 19,
-        out_specs=[anywhere] * 3 + [vmem] * 13,
-        scratch_shapes=[pltpu.SemaphoreType.DMA((3,))],
+        out_specs=[anywhere] * 3 + [vmem] + [anywhere] * 12,
+        scratch_shapes=[pltpu.VMEM(a.shape, F32) for a in state] + [pltpu.SemaphoreType.DMA((15,))],
         compiler_params=pltpu.CompilerParams(vmem_limit_bytes=32 * 2**20),
         name="closing",
     )(*results, *state)

time: 76.9 us -> 70.8 us (0.921)
  Pallas kernels: 75.7 us -> 69.6 us
    pallas_call x1, Pallas kernels: 71 us -> 65.1 us  [__call__(): pl.pallas_call(self.kernel, out_shape=[wide, wide, wide, pltpu.VMEM((256,...]
where the time goes in v3:
time: 70.8 us; the launch traced here: 70.7 us
  Pallas kernels  69.6 us (98%)
  between operations  1.03 us (1%)
    pallas_call x1, Pallas kernels, __call__(): pl.pallas_call(self.kernel, out_shape=[wide, wide, wide, pltpu.VMEM((256,...  65.1 us
    pallas_call x1, Pallas kernels, closing(): pl.pallas_call(functools.partial(closing_kernel, layer.cond_rows, layer.t...  4.52 us

profile of v3, /device:TPU:0, one launch (start us, length us, event | category | flops | bytes accessed | tf_op | source)
XLA Modules:
  0.0 70.7 jit_solution(2655210136230258179)
XLA Ops:
  0.7 0.0 copy-start.1
  0.7 0.0 copy-start.6
  0.7 0.0 copy-start.7
  0.7 0.0 copy-start
  0.7 0.0 copy-start.5
  0.7 0.0 copy-start.4
  0.7 0.0 copy-start.9
  0.7 0.0 copy-start.8
  0.7 0.0 copy-start.11
  0.7 0.0 copy-start.10
  0.8 0.0 copy-start.3
  0.8 0.0 copy-start.2
  0.8 65.1 %layer.1 = (bf16[3072,512]{1,0:T(8,128)(2,1)S(1)}, bf16[3072,512]{1,0:T(8,128)(2,1)S(1)}, bf16[3072,512]{1,0:T(8,128)(2,1)S(1)}, f32[256,128]{1,0:T(8,128)S(1)},...) custom-call(s32[1,8]{1,0:T(1,128)} %ids_in.1, s32[1,8]{1,0:T(1,128)} %starts_in.1, ...), custom_call_target="tpu_custom_call" | custom-call | tf_op jit(solution)/shard_map/layer/pallas_call | solution.py:799
  65.9 0.0 copy-done.1
  65.9 0.0 copy-done.6
  65.9 0.0 copy-done.7
  65.9 0.0 copy-done
  65.9 0.0 copy-done.5
  65.9 0.0 copy-done.4
  65.9 0.0 copy-done.9
  65.9 0.0 copy-done.8
  65.9 0.0 copy-done.11
  66.0 0.0 copy-done.10
  66.0 4.5 %closing.1 = (bf16[1,3072,512]{2,1,0:T(8,128)(2,1)}, bf16[1,3072,512]{2,1,0:T(8,128)(2,1)}, bf16[1,3072,512]{2,1,0:T(8,128)(2,1)}, f32[1,1]{1,0:T(1,128)}, f32[2...) custom-call(bf16[3072,512]{1,0:T(8,128)(2,1)S(1)} %get-tuple-element, ...), custom_call_target="tpu_custom_call" | custom-call | tf_op jit(solution)/shard_map/closing/pallas_call | solution.py:855
  (2 shorter events, 0.0 us)
Async XLA Ops:
  0.7 65.2 %copy-start.1 = (f32[128,128]{1,0:T(8,128)S(1)}, f32[128,128]{1,0:T(8,128)}, u32[]{:S(2)}) copy-start(f32[128,128]{1,0:T(8,128)} %refs_16_.1) | copy-start | bytes 196612
  0.7 65.2 %copy-start.6 = (f32[28,128]{1,0:T(8,128)S(1)}, f32[28,128]{1,0:T(8,128)}, u32[]{:S(2)}) copy-start(f32[28,128]{1,0:T(8,128)} %refs_13_.1) | copy-start | bytes 43012
  0.7 65.2 %copy-start.7 = (f32[20,128]{1,0:T(8,128)S(1)}, f32[20,128]{1,0:T(8,128)}, u32[]{:S(2)}) copy-start(f32[20,128]{1,0:T(8,128)} %refs_10_.1) | copy-start | bytes 30724
  0.7 65.2 %copy-start = (f32[256,128]{1,0:T(8,128)S(1)}, f32[256,128]{1,0:T(8,128)}, u32[]{:S(2)}) copy-start(f32[256,128]{1,0:T(8,128)} %refs_7_.1) | copy-start | bytes 393220
  0.7 65.2 %copy-start.5 = (f32[128,128]{1,0:T(8,128)S(1)}, f32[128,128]{1,0:T(8,128)}, u32[]{:S(2)}) copy-start(f32[128,128]{1,0:T(8,128)} %refs_18_.1) | copy-start | bytes 196612
  0.7 65.2 %copy-start.4 = (f32[128,128]{1,0:T(8,128)S(1)}, f32[128,128]{1,0:T(8,128)}, u32[]{:S(2)}) copy-start(f32[128,128]{1,0:T(8,128)} %refs_17_.1) | copy-start | bytes 196612
  0.7 65.2 %copy-start.9 = (f32[28,128]{1,0:T(8,128)S(1)}, f32[28,128]{1,0:T(8,128)}, u32[]{:S(2)}) copy-start(f32[28,128]{1,0:T(8,128)} %refs_15_.1) | copy-start | bytes 43012
  0.7 65.2 %copy-start.8 = (f32[28,128]{1,0:T(8,128)S(1)}, f32[28,128]{1,0:T(8,128)}, u32[]{:S(2)}) copy-start(f32[28,128]{1,0:T(8,128)} %refs_14_.1) | copy-start | bytes 43012
  0.7 65.2 %copy-start.11 = (f32[20,128]{1,0:T(8,128)S(1)}, f32[20,128]{1,0:T(8,128)}, u32[]{:S(2)}) copy-start(f32[20,128]{1,0:T(8,128)} %refs_12_.1) | copy-start | bytes 30724
  0.7 65.2 %copy-start.10 = (f32[20,128]{1,0:T(8,128)S(1)}, f32[20,128]{1,0:T(8,128)}, u32[]{:S(2)}) copy-start(f32[20,128]{1,0:T(8,128)} %refs_11_.1) | copy-start | bytes 30724
  0.8 65.2 %copy-start.3 = (f32[256,128]{1,0:T(8,128)S(1)}, f32[256,128]{1,0:T(8,128)}, u32[]{:S(2)}) copy-start(f32[256,128]{1,0:T(8,128)} %refs_9_.1) | copy-start | bytes 393220
  0.8 65.2 %copy-start.2 = (f32[256,128]{1,0:T(8,128)S(1)}, f32[256,128]{1,0:T(8,128)}, u32[]{:S(2)}) copy-start(f32[256,128]{1,0:T(8,128)} %refs_8_.1) | copy-start | bytes 393220
